TPU v7x, 512 devices: a whole 4x4x16 slice. The times are simulated.
512 devices in a mesh: gx: 16 (over z_lo, core), gy: 16 (over y, x), gz: 2 (over z_hi).
Axes of the slice: x: 4, y: 4, z: 16 (z_hi: 2, z_lo: 8; z = z_hi * 8 + z_lo), core: 2. Of those that a mesh axis runs over, the one named last changes fastest.
Arguments:
- log_range: float32 [32, 512, 2048], P('gz', 'gx', 'gy'), may hold values from -0.5 to 1.5
- sea_mask: int32 [32, 512, 2048], P('gz', 'gx', 'gy'), may hold values 0 or 1
- forcing: float32 [32, 512, 2048], P('gz', 'gx', 'gy'), may hold values from -24 to 24
- cotangent: float32 [32, 512, 2048], P('gz', 'gx', 'gy'), may hold values from -24 to 24
Outputs:
- iterate: float32 [32, 512, 2048], P('gz', 'gx', 'gy')
- range_grad: float32 [32, 512, 2048], P('gz', 'gx', 'gy')
All inputs are finite; a program needn't handle non-finite values. No bound on the sum of `sea_mask` on one device may be relied on, other than what follows from the above.
Results may differ from a plain program's by a relative error of at most 0.00002.
Values sent between devices are 32-bit elements; how exact they have to be, the bound alone decides.
A program may use at most 64 MiB of HBM per device.

v0:
```python
import jax
import jax.numpy as jnp
from jax import lax
from jax.sharding import PartitionSpec as P

SWEEPS = 4


relaxation = 0.9


def padded_2(shard, sides, width):
    for axis, dim in sides:
        size, length = (lax.axis_size(axis), shard.shape[dim])
        up = [(i, (i + 1) % size) for i in range(size - 1)]
        down = [(j, i) for i, j in up]
        last = lax.slice_in_dim(shard, length - width, length, axis=dim)
        initial = lax.slice_in_dim(shard, 0, width, axis=dim)
        before = lax.ppermute(last, axis, up)
        after = lax.ppermute(initial, axis, down)
        shard = jnp.concatenate([before, shard, after], axis=dim)
    return shard


def neighbours(padded):
    total = padded[2:, 1:-1, 1:-1] + padded[:-2, 1:-1, 1:-1]
    total = total + padded[1:-1, 2:, 1:-1] + padded[1:-1, :-2, 1:-1]
    total = total + padded[1:-1, 1:-1, 2:] + padded[1:-1, 1:-1, :-2]
    return total


def crop(field, margin):
    if margin == 0:
        return field
    return field[margin:-margin, margin:-margin, margin:-margin]


def forward_step(padded, margin, statics):
    sea, diagonal, source, depth_pad = statics
    outer_sea = crop(sea, depth_pad - 1 - margin)
    spread = neighbours(outer_sea * padded)
    inner = depth_pad - margin
    return (1.0 - relaxation) * crop(padded, 1) + relaxation * (
        crop(source, inner) + crop(sea, inner) * spread
    ) / crop(diagonal, inner)


def adjoint_step(padded, margin, statics):
    sea, diagonal, source, depth_pad = statics
    outer = depth_pad - 1 - margin
    scaled = crop(sea, outer) * relaxation * padded / crop(diagonal, outer)
    return (1.0 - relaxation) * crop(padded, 1) + crop(sea, depth_pad - margin) * neighbours(scaled)


def body(log_range, sea_mask, forcing, cotangent):
    sea_local = sea_mask.astype(jnp.float32)
    diagonal = sea_local * (6.0 + jnp.exp(-2.0 * log_range)) + (1.0 - sea_local)
    diagonal_wide, source_pad = (
        padded_2(diagonal, (("gx", 1), ("gy", 2), ("gz", 0)), SWEEPS),
        padded_2(forcing, (("gx", 1), ("gy", 2), ("gz", 0)), SWEEPS),
    )
    sea_pad = jnp.where(
        diagonal_wide > 3.0, jnp.ones_like(diagonal_wide), jnp.zeros_like(diagonal_wide)
    )
    diagonal_pad = jnp.maximum(diagonal_wide, 1.0)
    statics = (sea_pad, diagonal_pad, source_pad, SWEEPS)
    zeros = jnp.zeros_like(forcing)
    state = jnp.zeros_like(source_pad)
    forward_states = [zeros]
    for sweep_index in range(SWEEPS):
        margin = SWEEPS - 1 - sweep_index
        state = forward_step(state, margin, statics)
        forward_states.append(crop(state, margin))
    adjoint = padded_2(cotangent, (("gx", 1), ("gy", 2), ("gz", 0)), SWEEPS - 1)
    adjoints = [cotangent]
    for sweep_index in range(SWEEPS - 1):
        margin = SWEEPS - 2 - sweep_index
        adjoint = adjoint_step(adjoint, margin, statics)
        adjoints.append(crop(adjoint, margin))
    iterate = forward_states[-1]
    accumulated = jnp.zeros_like(forcing)
    for back in range(SWEEPS):
        level = SWEEPS - 1 - back
        accumulated = accumulated + adjoints[back] * (
            forward_states[level + 1] - (1.0 - relaxation) * forward_states[level]
        )
    range_grad = 2.0 * sea_local * jnp.exp(-2.0 * log_range) / diagonal * accumulated
    return (iterate, range_grad)


def solution(mesh):
    placed = (P("gz", "gx", "gy"), P("gz", "gx", "gy"), P("gz", "gx", "gy"), P("gz", "gx", "gy"))
    return jax.shard_map(
        body,
        mesh=mesh,
        in_specs=placed,
        out_specs=(P("gz", "gx", "gy"), P("gz", "gx", "gy")),
        check_vma=False,
    )
```

profile of v0, /device:TPU:40, one launch (start us, length us, event | category | flops | bytes accessed | tf_op | source)
XLA Modules:
  0.0 132.1 jit_solution(1696103667353648599)
XLA Ops:
  0.6 0.0 copy-start.2
  0.6 0.9 fusion.38
  1.6 1.9 %collective-permute-start = (f32[16,4,128]{2,1,0:T(4,128)S(1)}, f32[16,4,128]{2,1,0:T(4,128)S(1)}, u32[]{:S(2)}, u32[]{:S(2)}) collective-permute-start(f32[16,4,128]{2,1,0:T(4,128)S(1)} %get-tuple-element.37), channel_id=1, source_target_pairs={{0,32},{32,64},{64,96},{96,128},{128,160},{160,192},{192,224},{224... | collective-permute-start | bytes 98312 | tf_op jit(solution)/shard_map/ppermute | solution.py:19
  3.5 3.6 %collective-permute-start.1 = (f32[16,4,128]{2,1,0:T(4,128)S(1)}, f32[16,4,128]{2,1,0:T(4,128)S(1)}, u32[]{:S(2)}, u32[]{:S(2)}) collective-permute-start(f32[16,4,128]{2,1,0:T(4,128)S(1)} %get-tuple-element.38), channel_id=1, source_target_pairs={{32,0},{64,32},{96,64},{128,96},{160,128},{192,160},{224,192},{256... | collective-permute-start | bytes 98312 | tf_op jit(solution)/shard_map/ppermute | solution.py:20
  7.2 0.9 fusion.39
  8.0 2.2 %collective-permute-start.12 = (f32[16,3,128]{2,1,0:T(4,128)S(1)}, f32[16,3,128]{2,1,0:T(4,128)S(1)}, u32[]{:S(2)}, u32[]{:S(2)}) collective-permute-start(f32[16,3,128]{2,1,0:T(4,128)S(1)} %get-tuple-element.39), channel_id=1, source_target_pairs={{0,32},{32,64},{64,96},{96,128},{128,160},{160,192},{192,224},{224... | collective-permute-start | bytes 73736 | tf_op jit(solution)/shard_map/ppermute | solution.py:19
  10.3 0.0 copy-start.1
  10.3 3.5 %collective-permute-start.13 = (f32[16,3,128]{2,1,0:T(4,128)S(1)}, f32[16,3,128]{2,1,0:T(4,128)S(1)}, u32[]{:S(2)}, u32[]{:S(2)}) collective-permute-start(f32[16,3,128]{2,1,0:T(4,128)S(1)} %get-tuple-element.40), channel_id=1, source_target_pairs={{32,0},{64,32},{96,64},{128,96},{160,128},{192,160},{224,192},{256... | collective-permute-start | bytes 73736 | tf_op jit(solution)/shard_map/ppermute | solution.py:20
  13.8 0.0 copy-done.2
  13.8 1.0 subtract_add_fusion
  14.8 0.0 collective-permute-done.12
  14.8 0.5 collective-permute-done.13
  15.3 0.0 copy-done.1
  15.4 0.2 fusion.36
  15.5 3.4 %collective-permute-start.14 = (f32[16,38,3]{2,1,0:T(8,128)S(1)}, f32[16,38,3]{2,1,0:T(8,128)S(1)}, u32[]{:S(2)}, u32[]{:S(2)}) collective-permute-start(f32[16,38,3]{2,1,0:T(8,128)S(1)} %get-tuple-element.33), channel_id=1, source_target_pairs={{0,2},{2,4},{4,6},{6,8},{8,10},{10,12},{12,14},{14,16},{16,18},{18... | collective-permute-start | bytes 21896 | tf_op jit(solution)/shard_map/ppermute | solution.py:19
  19.0 4.6 %collective-permute-start.15 = (f32[16,38,3]{2,1,0:T(8,128)S(1)}, f32[16,38,3]{2,1,0:T(8,128)S(1)}, u32[]{:S(2)}, u32[]{:S(2)}) collective-permute-start(f32[16,38,3]{2,1,0:T(8,128)S(1)} %get-tuple-element.34), channel_id=1, source_target_pairs={{2,0},{4,2},{6,4},{8,6},{10,8},{12,10},{14,12},{16,14},{18,16},{20... | collective-permute-start | bytes 21896 | tf_op jit(solution)/shard_map/ppermute | solution.py:20
  23.5 3.4 %collective-permute-start.6 = (f32[16,4,128]{2,1,0:T(4,128)S(1)}, f32[16,4,128]{2,1,0:T(4,128)S(1)}, u32[]{:S(2)}, u32[]{:S(2)}) collective-permute-start(f32[16,4,128]{2,1,0:T(4,128)S(1)} %get-tuple-element.41), channel_id=1, source_target_pairs={{0,32},{32,64},{64,96},{96,128},{128,160},{160,192},{192,224},{224... | collective-permute-start | bytes 98312 | tf_op jit(solution)/shard_map/ppermute | solution.py:19
  26.9 2.1 %collective-permute-done.14 = f32[16,38,3]{2,1,0:T(8,128)S(1)} collective-permute-done((f32[16,38,3]{2,1,0:T(8,128)S(1)}, f32[16,38,3]{2,1,0:T(8,128)S(1)}, u32[]{:S(2)}, u32[]{:S(2)}) %collective-permute-start.14) | collective-permute-done | bytes 7328 | tf_op jit(solution)/shard_map/ppermute | solution.py:19
  29.1 1.9 %collective-permute-start.7 = (f32[16,4,128]{2,1,0:T(4,128)S(1)}, f32[16,4,128]{2,1,0:T(4,128)S(1)}, u32[]{:S(2)}, u32[]{:S(2)}) collective-permute-start(f32[16,4,128]{2,1,0:T(4,128)S(1)} %get-tuple-element.42), channel_id=1, source_target_pairs={{32,0},{64,32},{96,64},{128,96},{160,128},{192,160},{224,192},{256... | collective-permute-start | bytes 98312 | tf_op jit(solution)/shard_map/ppermute | solution.py:20
  31.0 0.0 collective-permute-done.15
  31.0 0.2 pad_maximum_fusion.20
  31.2 15.7 %collective-permute-start.16 = (f32[3,38,134]{2,1,0:T(8,128)S(1)}, f32[3,38,134]{2,1,0:T(8,128)S(1)}, u32[]{:S(2)}, u32[]{:S(2)}) collective-permute-start(f32[3,38,134]{2,1,0:T(8,128)S(1)} %get-tuple-element.27), channel_id=1, source_target_pairs={{0,1},{2,3},{4,5},{6,7},{8,9},{10,11},{12,13},{14,15},{16,17},{18,... | collective-permute-start | bytes 183320 | tf_op jit(solution)/shard_map/ppermute | solution.py:19
  46.9 0.0 collective-permute-done.6
  46.9 1.3 collective-permute-start.17
  48.2 0.0 collective-permute-done.7
  48.3 0.0 copy-start
  48.3 0.2 fusion.37
  48.5 2.8 %collective-permute-start.8 = (f32[16,40,4]{2,1,0:T(8,128)S(1)}, f32[16,40,4]{2,1,0:T(8,128)S(1)}, u32[]{:S(2)}, u32[]{:S(2)}) collective-permute-start(f32[16,40,4]{2,1,0:T(8,128)S(1)} %get-tuple-element.35), channel_id=1, source_target_pairs={{0,2},{2,4},{4,6},{6,8},{8,10},{10,12},{12,14},{14,16},{16,18},{18... | collective-permute-start | bytes 30728 | tf_op jit(solution)/shard_map/ppermute | solution.py:19
  51.3 0.0 collective-permute-done
  51.3 5.2 %collective-permute-start.9 = (f32[16,40,4]{2,1,0:T(8,128)S(1)}, f32[16,40,4]{2,1,0:T(8,128)S(1)}, u32[]{:S(2)}, u32[]{:S(2)}) collective-permute-start(f32[16,40,4]{2,1,0:T(8,128)S(1)} %get-tuple-element.36), channel_id=1, source_target_pairs={{2,0},{4,2},{6,4},{8,6},{10,8},{12,10},{14,12},{16,14},{18,16},{20... | collective-permute-start | bytes 30728 | tf_op jit(solution)/shard_map/ppermute | solution.py:20
  56.5 0.0 collective-permute-done.1
  56.5 0.0 copy-done
  56.6 0.2 fusion.35
  56.7 1.9 %collective-permute-start.2 = (f32[16,40,4]{2,1,0:T(8,128)S(1)}, f32[16,40,4]{2,1,0:T(8,128)S(1)}, u32[]{:S(2)}, u32[]{:S(2)}) collective-permute-start(f32[16,40,4]{2,1,0:T(8,128)S(1)} %get-tuple-element.31), channel_id=1, source_target_pairs={{0,2},{2,4},{4,6},{6,8},{8,10},{10,12},{12,14},{14,16},{16,18},{18... | collective-permute-start | bytes 30728 | tf_op jit(solution)/shard_map/ppermute | solution.py:19
  58.7 3.7 %collective-permute-done.8 = f32[16,40,4]{2,1,0:T(8,128)S(1)} collective-permute-done((f32[16,40,4]{2,1,0:T(8,128)S(1)}, f32[16,40,4]{2,1,0:T(8,128)S(1)}, u32[]{:S(2)}, u32[]{:S(2)}) %collective-permute-start.8) | collective-permute-done | bytes 10272 | tf_op jit(solution)/shard_map/ppermute | solution.py:19
  62.3 4.7 %collective-permute-start.3 = (f32[16,40,4]{2,1,0:T(8,128)S(1)}, f32[16,40,4]{2,1,0:T(8,128)S(1)}, u32[]{:S(2)}, u32[]{:S(2)}) collective-permute-start(f32[16,40,4]{2,1,0:T(8,128)S(1)} %get-tuple-element.32), channel_id=1, source_target_pairs={{2,0},{4,2},{6,4},{8,6},{10,8},{12,10},{14,12},{16,14},{18,16},{20... | collective-permute-start | bytes 30728 | tf_op jit(solution)/shard_map/ppermute | solution.py:20
  67.1 0.0 collective-permute-done.9
  67.1 0.2 pad_maximum_fusion.10
  67.3 13.1 %collective-permute-start.10 = (f32[4,40,136]{2,1,0:T(8,128)S(1)}, f32[4,40,136]{2,1,0:T(8,128)S(1)}, u32[]{:S(2)}, u32[]{:S(2)}) collective-permute-start(f32[4,40,136]{2,1,0:T(8,128)S(1)} %get-tuple-element.29), channel_id=1, source_target_pairs={{0,1},{2,3},{4,5},{6,7},{8,9},{10,11},{12,13},{14,15},{16,17},{18,... | collective-permute-start | bytes 261128 | tf_op jit(solution)/shard_map/ppermute | solution.py:19
  80.4 0.0 collective-permute-done.2
  80.4 1.3 collective-permute-start.11
  81.7 0.0 collective-permute-done.3
  81.8 0.2 pad_maximum_fusion.15
  82.0 13.3 %collective-permute-start.4 = (f32[4,40,136]{2,1,0:T(8,128)S(1)}, f32[4,40,136]{2,1,0:T(8,128)S(1)}, u32[]{:S(2)}, u32[]{:S(2)}) collective-permute-start(f32[4,40,136]{2,1,0:T(8,128)S(1)} %get-tuple-element.25), channel_id=1, source_target_pairs={{0,1},{2,3},{4,5},{6,7},{8,9},{10,11},{12,13},{14,15},{16,17},{18,... | collective-permute-start | bytes 261128 | tf_op jit(solution)/shard_map/ppermute | solution.py:19
  95.3 0.0 collective-permute-done.10
  95.3 1.5 %collective-permute-start.5 = (f32[4,40,136]{2,1,0:T(8,128)S(1)}, f32[4,40,136]{2,1,0:T(8,128)S(1)}, u32[]{:S(2)}, u32[]{:S(2)}) collective-permute-start(f32[4,40,136]{2,1,0:T(8,128)S(1)} %get-tuple-element.26), channel_id=1, source_target_pairs={{1,0},{3,2},{5,4},{7,6},{9,8},{11,10},{13,12},{15,14},{17,16},{19,... | collective-permute-start | bytes 261128 | tf_op jit(solution)/shard_map/ppermute | solution.py:20
  96.8 4.2 %collective-permute-done.11 = f32[4,40,136]{2,1,0:T(8,128)S(1)} collective-permute-done((f32[4,40,136]{2,1,0:T(8,128)S(1)}, f32[4,40,136]{2,1,0:T(8,128)S(1)}, u32[]{:S(2)}, u32[]{:S(2)}) %collective-permute-start.11) | collective-permute-done | bytes 87072 | tf_op jit(solution)/shard_map/ppermute | solution.py:20
  101.0 0.4 broadcast_multiply_fusion
  101.4 4.3 %collective-permute-done.4 = f32[4,40,136]{2,1,0:T(8,128)S(1)} collective-permute-done((f32[4,40,136]{2,1,0:T(8,128)S(1)}, f32[4,40,136]{2,1,0:T(8,128)S(1)}, u32[]{:S(2)}, u32[]{:S(2)}) %collective-permute-start.4) | collective-permute-done | bytes 87072 | tf_op jit(solution)/shard_map/ppermute | solution.py:19
  105.7 15.2 %collective-permute-done.5 = f32[4,40,136]{2,1,0:T(8,128)S(1)} collective-permute-done((f32[4,40,136]{2,1,0:T(8,128)S(1)}, f32[4,40,136]{2,1,0:T(8,128)S(1)}, u32[]{:S(2)}, u32[]{:S(2)}) %collective-permute-start.5) | collective-permute-done | bytes 87072 | tf_op jit(solution)/shard_map/ppermute | solution.py:20
  120.9 0.4 pad_maximum_fusion
  121.3 0.0 collective-permute-done.16
  121.3 0.0 collective-permute-done.17
  121.4 2.3 %slice_multiply_fusion.2 = (f32[22,38,134]{2,1,0:T(8,128)S(1)}, f32[22,38,134]{2,1,0:T(8,128)S(1)}, f32[22,38,134]{2,1,0:T(8,128)S(1)}, f32[22,38,134]{2,1,0:T(8,128)S(1)}) fusion(f32[24,40,136]{2,1,0:T(8,128)S(1)} %get-tuple-element.17, f32[24,40,136]{2,1,0:T(8,128)S(1)} %get-tuple-element.24, f32[24,40,136]{2,1,0:T(8,128)S(1)} %get-tuple-element.16, ...), kind=kLoop, calls=%fused_computation.34 | loop fusion | flops 2128456 | bytes 6273344 | tf_op jit(solution)/shard_map/mul | solution.py:41
  123.7 3.3 %slice_multiply_fusion.5 = (f32[20,36,132]{2,1,0:T(8,128)S(1)}, f32[20,36,132]{2,1,0:T(8,128)S(1)}, f32[20,36,132]{2,1,0:T(8,128)S(1)}, f32[20,36,132]{2,1,0:T(8,128)S(1)}) fusion(f32[24,40,136]{2,1,0:T(8,128)S(1)} %get-tuple-element.17, f32[24,40,136]{2,1,0:T(8,128)S(1)} %get-tuple-element.24, f32[22,38,134]{2,1,0:T(8,128)S(1)} %get-tuple-element.14, ...), kind=kLoop, calls=%fused_computation.55 | loop fusion | flops 2185920 | bytes 7983360 | tf_op jit(solution)/shard_map/mul | solution.py:41
  127.0 0.0 copy-start.3
  127.0 3.0 %slice_multiply_fusion.6 = (f32[18,34,130]{2,1,0:T(8,128)S(1)}, f32[18,34,130]{2,1,0:T(8,128)S(1)}, f32[18,34,130]{2,1,0:T(8,128)S(1)}, f32[18,34,130]{2,1,0:T(8,128)S(1)}) fusion(f32[24,40,136]{2,1,0:T(8,128)S(1)} %get-tuple-element.17, f32[24,40,136]{2,1,0:T(8,128)S(1)} %get-tuple-element.24, f32[20,36,132]{2,1,0:T(8,128)S(1)} %get-tuple-element.12, ...), kind=kLoop, calls=%fused_computation.56 | loop fusion | flops 1829880 | bytes 6683040 | tf_op jit(solution)/shard_map/mul | solution.py:41
  130.0 0.0 copy-done.3
  130.0 2.1 %fusion.22 = (f32[16,32,128]{2,1,0:T(8,128)}, f32[16,32,128]{2,1,0:T(8,128)}) fusion(f32[18,34,130]{2,1,0:T(8,128)S(1)} %get-tuple-element.18, f32[20,36,132]{2,1,0:T(8,128)S(1)} %get-tuple-element.21, f32[18,34,130]{2,1,0:T(8,128)S(1)} %get-tuple-element.19, f32[22,38,134]{2,1,0:T(8,128)S(1)} %get-tuple-element.15, ...), kind=kLoop, calls=%fused_computation.67 | loop fusion | flops 2686976 | bytes 6553600 | tf_op jit(solution)/shard_map/mul | solution.py:87
  (4 shorter events, 0.1 us)
Async XLA Ops:
  0.6 13.1 %copy-start.2 = (s32[16,32,128]{2,1,0:T(8,128)S(1)}, s32[16,32,128]{2,1,0:T(8,128)}, u32[]{:S(2)}) copy-start(s32[16,32,128]{2,1,0:T(8,128)} %param.5) | copy-start | bytes 786436
  1.6 49.7 %collective-permute-start = (f32[16,4,128]{2,1,0:T(4,128)S(1)}, f32[16,4,128]{2,1,0:T(4,128)S(1)}, u32[]{:S(2)}, u32[]{:S(2)}) collective-permute-start(f32[16,4,128]{2,1,0:T(4,128)S(1)} %get-tuple-element.37), channel_id=1, source_target_pairs={{0,32},{32,64},{64,96},{96,128},{128,160},{160,192},{192,224},{224... | collective-permute-start | bytes 98312 | tf_op jit(solution)/shard_map/ppermute | solution.py:19
  3.5 53.0 %collective-permute-start.1 = (f32[16,4,128]{2,1,0:T(4,128)S(1)}, f32[16,4,128]{2,1,0:T(4,128)S(1)}, u32[]{:S(2)}, u32[]{:S(2)}) collective-permute-start(f32[16,4,128]{2,1,0:T(4,128)S(1)} %get-tuple-element.38), channel_id=1, source_target_pairs={{32,0},{64,32},{96,64},{128,96},{160,128},{192,160},{224,192},{256... | collective-permute-start | bytes 98312 | tf_op jit(solution)/shard_map/ppermute | solution.py:20
  8.0 6.8 %collective-permute-start.12 = (f32[16,3,128]{2,1,0:T(4,128)S(1)}, f32[16,3,128]{2,1,0:T(4,128)S(1)}, u32[]{:S(2)}, u32[]{:S(2)}) collective-permute-start(f32[16,3,128]{2,1,0:T(4,128)S(1)} %get-tuple-element.39), channel_id=1, source_target_pairs={{0,32},{32,64},{64,96},{96,128},{128,160},{160,192},{192,224},{224... | collective-permute-start | bytes 73736 | tf_op jit(solution)/shard_map/ppermute | solution.py:19
  10.3 5.1 %copy-start.1 = (f32[16,32,128]{2,1,0:T(8,128)S(1)}, f32[16,32,128]{2,1,0:T(8,128)}, u32[]{:S(2)}) copy-start(f32[16,32,128]{2,1,0:T(8,128)} %param.7) | copy-start | bytes 786436
  10.3 5.1 %collective-permute-start.13 = (f32[16,3,128]{2,1,0:T(4,128)S(1)}, f32[16,3,128]{2,1,0:T(4,128)S(1)}, u32[]{:S(2)}, u32[]{:S(2)}) collective-permute-start(f32[16,3,128]{2,1,0:T(4,128)S(1)} %get-tuple-element.40), channel_id=1, source_target_pairs={{32,0},{64,32},{96,64},{128,96},{160,128},{192,160},{224,192},{256... | collective-permute-start | bytes 73736 | tf_op jit(solution)/shard_map/ppermute | solution.py:20
  15.5 13.5 %collective-permute-start.14 = (f32[16,38,3]{2,1,0:T(8,128)S(1)}, f32[16,38,3]{2,1,0:T(8,128)S(1)}, u32[]{:S(2)}, u32[]{:S(2)}) collective-permute-start(f32[16,38,3]{2,1,0:T(8,128)S(1)} %get-tuple-element.33), channel_id=1, source_target_pairs={{0,2},{2,4},{4,6},{6,8},{8,10},{10,12},{12,14},{14,16},{16,18},{18... | collective-permute-start | bytes 21896 | tf_op jit(solution)/shard_map/ppermute | solution.py:19
  19.0 12.0 %collective-permute-start.15 = (f32[16,38,3]{2,1,0:T(8,128)S(1)}, f32[16,38,3]{2,1,0:T(8,128)S(1)}, u32[]{:S(2)}, u32[]{:S(2)}) collective-permute-start(f32[16,38,3]{2,1,0:T(8,128)S(1)} %get-tuple-element.34), channel_id=1, source_target_pairs={{2,0},{4,2},{6,4},{8,6},{10,8},{12,10},{14,12},{16,14},{18,16},{20... | collective-permute-start | bytes 21896 | tf_op jit(solution)/shard_map/ppermute | solution.py:20
  23.5 23.4 %collective-permute-start.6 = (f32[16,4,128]{2,1,0:T(4,128)S(1)}, f32[16,4,128]{2,1,0:T(4,128)S(1)}, u32[]{:S(2)}, u32[]{:S(2)}) collective-permute-start(f32[16,4,128]{2,1,0:T(4,128)S(1)} %get-tuple-element.41), channel_id=1, source_target_pairs={{0,32},{32,64},{64,96},{96,128},{128,160},{160,192},{192,224},{224... | collective-permute-start | bytes 98312 | tf_op jit(solution)/shard_map/ppermute | solution.py:19
  29.1 19.2 %collective-permute-start.7 = (f32[16,4,128]{2,1,0:T(4,128)S(1)}, f32[16,4,128]{2,1,0:T(4,128)S(1)}, u32[]{:S(2)}, u32[]{:S(2)}) collective-permute-start(f32[16,4,128]{2,1,0:T(4,128)S(1)} %get-tuple-element.42), channel_id=1, source_target_pairs={{32,0},{64,32},{96,64},{128,96},{160,128},{192,160},{224,192},{256... | collective-permute-start | bytes 98312 | tf_op jit(solution)/shard_map/ppermute | solution.py:20
  31.2 90.1 %collective-permute-start.16 = (f32[3,38,134]{2,1,0:T(8,128)S(1)}, f32[3,38,134]{2,1,0:T(8,128)S(1)}, u32[]{:S(2)}, u32[]{:S(2)}) collective-permute-start(f32[3,38,134]{2,1,0:T(8,128)S(1)} %get-tuple-element.27), channel_id=1, source_target_pairs={{0,1},{2,3},{4,5},{6,7},{8,9},{10,11},{12,13},{14,15},{16,17},{18,... | collective-permute-start | bytes 183320 | tf_op jit(solution)/shard_map/ppermute | solution.py:19
  46.9 74.4 %collective-permute-start.17 = (f32[3,38,134]{2,1,0:T(8,128)S(1)}, f32[3,38,134]{2,1,0:T(8,128)S(1)}, u32[]{:S(2)}, u32[]{:S(2)}) collective-permute-start(f32[3,38,134]{2,1,0:T(8,128)S(1)} %get-tuple-element.28), channel_id=1, source_target_pairs={{1,0},{3,2},{5,4},{7,6},{9,8},{11,10},{13,12},{15,14},{17,16},{19,... | collective-permute-start | bytes 183320 | tf_op jit(solution)/shard_map/ppermute | solution.py:20
  48.3 8.2 %copy-start = (f32[16,32,128]{2,1,0:T(8,128)S(1)}, f32[16,32,128]{2,1,0:T(8,128)}, u32[]{:S(2)}) copy-start(f32[16,32,128]{2,1,0:T(8,128)} %param.6) | copy-start | bytes 786436
  48.5 13.8 %collective-permute-start.8 = (f32[16,40,4]{2,1,0:T(8,128)S(1)}, f32[16,40,4]{2,1,0:T(8,128)S(1)}, u32[]{:S(2)}, u32[]{:S(2)}) collective-permute-start(f32[16,40,4]{2,1,0:T(8,128)S(1)} %get-tuple-element.35), channel_id=1, source_target_pairs={{0,2},{2,4},{4,6},{6,8},{8,10},{10,12},{12,14},{14,16},{16,18},{18... | collective-permute-start | bytes 30728 | tf_op jit(solution)/shard_map/ppermute | solution.py:19
  51.3 15.8 %collective-permute-start.9 = (f32[16,40,4]{2,1,0:T(8,128)S(1)}, f32[16,40,4]{2,1,0:T(8,128)S(1)}, u32[]{:S(2)}, u32[]{:S(2)}) collective-permute-start(f32[16,40,4]{2,1,0:T(8,128)S(1)} %get-tuple-element.36), channel_id=1, source_target_pairs={{2,0},{4,2},{6,4},{8,6},{10,8},{12,10},{14,12},{16,14},{18,16},{20... | collective-permute-start | bytes 30728 | tf_op jit(solution)/shard_map/ppermute | solution.py:20
  56.7 23.7 %collective-permute-start.2 = (f32[16,40,4]{2,1,0:T(8,128)S(1)}, f32[16,40,4]{2,1,0:T(8,128)S(1)}, u32[]{:S(2)}, u32[]{:S(2)}) collective-permute-start(f32[16,40,4]{2,1,0:T(8,128)S(1)} %get-tuple-element.31), channel_id=1, source_target_pairs={{0,2},{2,4},{4,6},{6,8},{8,10},{10,12},{12,14},{14,16},{16,18},{18... | collective-permute-start | bytes 30728 | tf_op jit(solution)/shard_map/ppermute | solution.py:19
  62.3 19.4 %collective-permute-start.3 = (f32[16,40,4]{2,1,0:T(8,128)S(1)}, f32[16,40,4]{2,1,0:T(8,128)S(1)}, u32[]{:S(2)}, u32[]{:S(2)}) collective-permute-start(f32[16,40,4]{2,1,0:T(8,128)S(1)} %get-tuple-element.32), channel_id=1, source_target_pairs={{2,0},{4,2},{6,4},{8,6},{10,8},{12,10},{14,12},{16,14},{18,16},{20... | collective-permute-start | bytes 30728 | tf_op jit(solution)/shard_map/ppermute | solution.py:20
  67.3 28.0 %collective-permute-start.10 = (f32[4,40,136]{2,1,0:T(8,128)S(1)}, f32[4,40,136]{2,1,0:T(8,128)S(1)}, u32[]{:S(2)}, u32[]{:S(2)}) collective-permute-start(f32[4,40,136]{2,1,0:T(8,128)S(1)} %get-tuple-element.29), channel_id=1, source_target_pairs={{0,1},{2,3},{4,5},{6,7},{8,9},{10,11},{12,13},{14,15},{16,17},{18,... | collective-permute-start | bytes 261128 | tf_op jit(solution)/shard_map/ppermute | solution.py:19
  80.4 20.6 %collective-permute-start.11 = (f32[4,40,136]{2,1,0:T(8,128)S(1)}, f32[4,40,136]{2,1,0:T(8,128)S(1)}, u32[]{:S(2)}, u32[]{:S(2)}) collective-permute-start(f32[4,40,136]{2,1,0:T(8,128)S(1)} %get-tuple-element.30), channel_id=1, source_target_pairs={{1,0},{3,2},{5,4},{7,6},{9,8},{11,10},{13,12},{15,14},{17,16},{19,... | collective-permute-start | bytes 261128 | tf_op jit(solution)/shard_map/ppermute | solution.py:20
  82.0 23.7 %collective-permute-start.4 = (f32[4,40,136]{2,1,0:T(8,128)S(1)}, f32[4,40,136]{2,1,0:T(8,128)S(1)}, u32[]{:S(2)}, u32[]{:S(2)}) collective-permute-start(f32[4,40,136]{2,1,0:T(8,128)S(1)} %get-tuple-element.25), channel_id=1, source_target_pairs={{0,1},{2,3},{4,5},{6,7},{8,9},{10,11},{12,13},{14,15},{16,17},{18,... | collective-permute-start | bytes 261128 | tf_op jit(solution)/shard_map/ppermute | solution.py:19
  95.3 25.7 %collective-permute-start.5 = (f32[4,40,136]{2,1,0:T(8,128)S(1)}, f32[4,40,136]{2,1,0:T(8,128)S(1)}, u32[]{:S(2)}, u32[]{:S(2)}) collective-permute-start(f32[4,40,136]{2,1,0:T(8,128)S(1)} %get-tuple-element.26), channel_id=1, source_target_pairs={{1,0},{3,2},{5,4},{7,6},{9,8},{11,10},{13,12},{15,14},{17,16},{19,... | collective-permute-start | bytes 261128 | tf_op jit(solution)/shard_map/ppermute | solution.py:20
  127.0 3.0 %copy-start.3 = (f32[16,32,128]{2,1,0:T(8,128)S(1)}, f32[16,32,128]{2,1,0:T(8,128)}, u32[]{:S(2)}) copy-start(f32[16,32,128]{2,1,0:T(8,128)} %param.4) | copy-start | bytes 786436
where the time goes:
time: 133 us; the launch traced here: 132 us
  starting transfers between devices  85.3 us (64%)
  waiting for transfers between devices  30.1 us (23%)
  other arithmetic  13.3 us (10%)
  local copies, waits for them, and re-layouts  2.34 us (2%)
    ppermute x9, starting transfers between devices, padded_2(): before = lax.ppermute(last, axis, up)  57.8 us
    ppermute x9, starting transfers between devices, padded_2(): after = lax.ppermute(initial, axis, down)  27.6 us
    ppermute x9, waiting for transfers between devices, padded_2(): after = lax.ppermute(initial, axis, down)  20 us
    ppermute x9, waiting for transfers between devices, padded_2(): before = lax.ppermute(last, axis, up)  10.1 us
    mul x4, other arithmetic, forward_step(): spread = neighbours(outer_sea * padded)  9.01 us
  transfers between devices with their start and end apart: 18, of which 6 were waited for; matrix products, arithmetic and copies ran while one was open for 3% of the time, Pallas kernels for 0%

commit v1 on v0

v1 whole, which is shorter than its diff:
```python
import functools

import jax
import jax.numpy as jnp
from jax import lax
from jax.experimental import pallas as pl
from jax.experimental.pallas import tpu as pltpu
from jax.sharding import PartitionSpec as P

MESH = pl.DeviceIdType.MESH
RELAX = 0.9
KEEP = 1.0 - RELAX
LAND = RELAX * (1.0 + KEEP + KEEP * KEEP + KEEP * KEEP * KEEP)
OWN = pl.ds(8, 32)


def roll(value, shift, axis):
    size = value.shape[axis]
    shift = shift % size
    return pltpu.roll(value, shift, axis) if shift else value


def stencil_full(ref, i):
    lane = lax.broadcasted_iota(jnp.int32, (48, 128), 1)
    first, last = lane == 0, lane == 127
    c0, c1 = ref[i, 0], ref[i, 1]
    r0, r1 = roll(c0, 1, 1), roll(c1, 1, 1)
    l0, l1 = roll(c0, -1, 1), roll(c1, -1, 1)
    n0 = ref[i - 1, 0] + ref[i + 1, 0] + (roll(c0, 1, 0) + roll(c0, -1, 0))
    n1 = ref[i - 1, 1] + ref[i + 1, 1] + (roll(c1, 1, 0) + roll(c1, -1, 0))
    n0 = n0 + jnp.where(first, r1, r0) + jnp.where(last, l1, l0)
    n1 = n1 + jnp.where(first, r0, r1) + jnp.where(last, l0, l1)
    return (c0, c1), (n0, n1)


def stencil_own(ref, i):
    lane = lax.broadcasted_iota(jnp.int32, (32, 128), 1)
    c = ref[i, 0]
    own = c[8:40]
    side = ref[i, 1, OWN]
    n = ref[i - 1, 0, OWN] + ref[i + 1, 0, OWN]
    n = n + (roll(c, 1, 0)[8:40] + roll(c, -1, 0)[8:40])
    n = n + jnp.where(lane == 0, roll(side, 1, 1), roll(own, 1, 1))
    n = n + jnp.where(lane == 127, roll(side, -1, 1), roll(own, -1, 1))
    return own, n


def kernel(sizes, lr_h, m_h, f_h, c_h, it_h, rg_h,
           lr, ms, fo, co, it, rg, a_, u1, u2, u3, w0, w1, w2,
           xs, xr, ys, yr, zs, zr, gs, gr, in_sem, out_sem, sem):
    nx, ny = sizes
    gz, gx, gy = lax.axis_index("gz"), lax.axis_index("gx"), lax.axis_index("gy")
    has = [gx > 0, gx < nx - 1, gy > 0, gy < ny - 1]
    to = [{"gx": gx - 1}, {"gx": gx + 1}, {"gy": gy - 1}, {"gy": gy + 1}]
    partner = {"gz": 1 - gz}

    barrier = pltpu.get_barrier_semaphore()
    pl.semaphore_signal(barrier, inc=1, device_id=partner, device_id_type=MESH)
    for here, device in zip(has, to):
        @pl.when(here)
        def _():
            pl.semaphore_signal(barrier, inc=1, device_id=device, device_id_type=MESH)

    loads = [pltpu.make_async_copy(h, v, in_sem.at[i]) for i, (h, v) in enumerate(((lr_h, lr), (m_h, ms), (f_h, fo), (c_h, co)))]
    for load in loads:
        load.start()

    def remote(src, dst, i, device):
        return pltpu.make_async_remote_copy(src_ref=src, dst_ref=dst, send_sem=sem.at[0, i], recv_sem=sem.at[1, i],
                                            device_id=device, device_id_type=MESH)

    xcopy = [remote(xs.at[0], xr.at[0], 0, to[0]), remote(xs.at[1], xr.at[1], 1, to[1])]
    ycopy = [remote(ys.at[0], yr.at[0], 2, to[2]), remote(ys.at[1], yr.at[1], 3, to[3])]
    zcopy = remote(zs, zr, 4, partner)
    gcopy = remote(gs, gr, 5, partner)

    def source(i):
        return jnp.where(gz == 0, i, 15 - i)

    row8 = lax.broadcasted_iota(jnp.int32, (8, 128), 0)
    lane8 = lax.broadcasted_iota(jnp.int32, (8, 128), 1)
    lane48 = lax.broadcasted_iota(jnp.int32, (48, 128), 1)
    zero = jnp.zeros((48, 128), jnp.float32)
    for ref in (u1, u2, u3, w0, w1, w2):
        ref[0, 0] = zero
        ref[0, 1] = zero
    for load in loads:
        load.wait()

    def prepare(i, _):
        z = source(i)
        mask = ms[z].astype(jnp.float32)
        inverse = 1.0 / (mask * (6.0 + jnp.exp(-2.0 * lr[z])) + (1.0 - mask))
        weight = RELAX * mask * inverse
        u, w = weight * fo[z], weight * co[z]
        a_[i + 1, 0, OWN] = weight
        u1[i + 1, 0, OWN] = u
        w0[i + 1, 0, OWN] = w
        up_u, up_w, up_a = u[:8], w[:8], weight[:8]
        dn_u, dn_w, dn_a = u[24:], w[24:], weight[24:]
        xs[0, i] = jnp.where(row8 < 3, up_u, jnp.where(row8 < 6, roll(up_w, 3, 0), roll(up_a, 6, 0)))
        xs[1, i] = jnp.where(row8 >= 5, dn_u, jnp.where(row8 >= 2, roll(dn_w, -3, 0), roll(dn_a, -6, 0)))
        return 0

    lax.fori_loop(0, 16, prepare, 0)
    for j in range(3):
        zs[j] = u1[16 - j, 0, OWN]
        zs[3 + j] = w0[16 - j, 0, OWN]
    for j in range(2):
        zs[6 + j] = a_[16 - j, 0, OWN]

    pl.semaphore_wait(barrier, 1 + sum(h.astype(jnp.int32) for h in has))
    for here, copy in zip(has[:2], xcopy):
        @pl.when(here)
        def _():
            copy.start()
    zcopy.start()

    for here, copy in zip((has[1], has[0]), xcopy):
        @pl.when(here)
        def _():
            copy.wait_recv()

    def x_halo(i, carry):
        right, left = carry
        low = jnp.where(has[1], xr[0, i], 0.0)
        top = jnp.where(has[0], xr[1, i], 0.0)
        u1[i + 1, 0, pl.ds(40, 8)] = low
        w0[i + 1, 0, pl.ds(40, 8)] = roll(low, -3, 0)
        a_[i + 1, 0, pl.ds(40, 8)] = roll(low, -6, 0)
        u1[i + 1, 0, pl.ds(0, 8)] = top
        w0[i + 1, 0, pl.ds(0, 8)] = roll(top, 3, 0)
        a_[i + 1, 0, pl.ds(0, 8)] = roll(top, 6, 0)
        u, w, weight = u1[i + 1, 0], w0[i + 1, 0], a_[i + 1, 0]
        to_right = jnp.where(lane48 < 3, roll(u, 3, 1), jnp.where(lane48 < 6, roll(w, 6, 1), roll(weight, 8, 1)))
        to_left = jnp.where(lane48 < 3, u, jnp.where(lane48 < 6, roll(w, 3, 1), roll(weight, 6, 1)))
        right = jnp.where(lane48 < 8, to_right, roll(right, 8, 1))
        left = jnp.where(lane48 < 8, to_left, roll(left, 8, 1))
        return right, left

    right, left = lax.fori_loop(0, 16, x_halo, (zero, zero))
    ys[1] = right
    ys[0] = left
    for here, copy in zip(has[2:], ycopy):
        @pl.when(here)
        def _():
            copy.start()
    for here, copy in zip((has[3], has[2]), ycopy):
        @pl.when(here)
        def _():
            copy.wait_recv()

    def y_halo(j, carry):
        left, right = carry
        i = 16 - j
        low = lane48 < 64
        u1[i, 1] = jnp.where(low, right, roll(left, -3, 1))
        w0[i, 1] = jnp.where(low, roll(right, -3, 1), roll(left, -6, 1))
        a_[i, 1] = jnp.where(low, roll(right, -6, 1), roll(left, -8, 1))
        return roll(left, -8, 1), roll(right, -8, 1)

    carry = (jnp.where(has[2], yr[1], 0.0), jnp.where(has[3], yr[0], 0.0))
    carry = lax.fori_loop(0, 3, y_halo, carry)

    ring = ((u1, 16, 2), (w0, 16, 2), (u1, 15, 1), (w0, 15, 1), (a_, 16, 1))
    top, low, columns = None, None, None
    at = 0
    for ref, i, depth in ring:
        t = roll(ref[i, 0, pl.ds(0, 8)], -at, 0)
        b = roll(ref[i, 0, pl.ds(40, 8)], at, 0)
        top = t if top is None else jnp.where(row8 < 8 - at, t, top)
        low = b if low is None else jnp.where(row8 >= at, b, low)
        at += depth
    for k in range(6):
        part, at = None, 0
        for ref, i, depth in ring:
            c = roll(ref[i, 1, pl.ds(8 * k, 8)], at + depth + 16 * k, 1)
            part = c if part is None else jnp.where(lane8 >= at + 16 * k, c, part)
            at += 2 * depth
        columns = part if columns is None else jnp.where(lane8 >= 16 * k, part, columns)
    gs[0], gs[1], gs[2] = top, low, columns
    gcopy.start()
    lax.fori_loop(3, 16, y_halo, carry)

    def sweep(old_u, new_u, old_w, new_w):
        def run(i, _):
            (c0, c1), (n0, n1) = stencil_full(old_u, i)
            new_u[i, 0] = KEEP * c0 + u1[i, 0] + a_[i, 0] * n0
            new_u[i, 1] = KEEP * c1 + u1[i, 1] + a_[i, 1] * n1
            (c0, c1), (n0, n1) = stencil_full(old_w, i)
            new_w[i, 0] = KEEP * c0 + a_[i, 0] * n0
            new_w[i, 1] = KEEP * c1 + a_[i, 1] * n1
            return 0
        return run

    def finish(i, _):
        z = source(i - 1)
        weight, s1 = a_[i, 0, OWN], u1[i, 0, OWN]
        c, n = stencil_own(u3, i)
        s4 = s1 + weight * n
        b, n = stencil_own(w2, i)
        w3 = KEEP * b + weight * n
        second = u2[i, 0, OWN]
        total = w0[i, 0, OWN] * s4 + w1[i, 0, OWN] * (c - KEEP * second) + b * (second - KEEP * s1) + w3 * s1
        rg[z] = (2.0 / RELAX) * jnp.exp(-2.0 * lr[z]) * total
        it[z] = jnp.where(ms[z] > 0, KEEP * c + s4, LAND * fo[z])
        return 0

    first = sweep(u1, u2, w0, w1)
    second = sweep(u2, u3, w1, w2)
    lax.fori_loop(1, 16, first, 0)
    lax.fori_loop(1, 15, second, 0)
    lax.fori_loop(1, 14, finish, 0)

    bulk, edge = pl.ds(3 * gz, 13), pl.ds(13 * (1 - gz), 3)
    stores = [pltpu.make_async_copy(v.at[part], h.at[part], out_sem.at[i])
              for i, (v, h, part) in enumerate(((it, it_h, bulk), (rg, rg_h, bulk), (it, it_h, edge), (rg, rg_h, edge)))]
    stores[0].start()
    stores[1].start()

    zcopy.wait_recv()
    for j in range(3):
        u1[17 + j, 0, OWN] = zr[j]
        w0[17 + j, 0, OWN] = zr[3 + j]
    for j in range(2):
        a_[17 + j, 0, OWN] = zr[6 + j]
    gcopy.wait_recv()
    top, low, columns = gr[0], gr[1], gr[2]
    at = 0
    for ref, i, depth in ring:
        ref[33 - i, 0, pl.ds(0, 8)] = roll(top, at, 0)
        ref[33 - i, 0, pl.ds(40, 8)] = roll(low, -at, 0)
        at += depth
    for k in range(6):
        at = 0
        for ref, i, depth in ring:
            ref[33 - i, 1, pl.ds(8 * k, 8)] = roll(columns, -(at + depth + 16 * k), 1)
            at += 2 * depth

    lax.fori_loop(16, 19, first, 0)
    lax.fori_loop(15, 18, second, 0)
    lax.fori_loop(14, 17, finish, 0)
    stores[2].start()
    stores[3].start()

    for here, copy in zip(has, xcopy + ycopy):
        @pl.when(here)
        def _():
            copy.wait_send()
    zcopy.wait_send()
    gcopy.wait_send()
    for store in stores:
        store.wait()


def solution(mesh):
    sizes = mesh.shape["gx"], mesh.shape["gy"]
    spec = P("gz", "gx", "gy")

    def body(log_range, sea_mask, forcing, cotangent):
        block = log_range.shape
        f32 = jnp.float32
        field = pltpu.VMEM((20, 2, 48, 128), f32)
        return pl.pallas_call(
            functools.partial(kernel, sizes),
            out_shape=[jax.ShapeDtypeStruct(block, f32)] * 2,
            in_specs=[pl.BlockSpec(memory_space=pl.ANY)] * 4,
            out_specs=[pl.BlockSpec(memory_space=pl.ANY)] * 2,
            scratch_shapes=[
                pltpu.VMEM(block, f32), pltpu.VMEM(block, jnp.int32), pltpu.VMEM(block, f32), pltpu.VMEM(block, f32),
                pltpu.VMEM(block, f32), pltpu.VMEM(block, f32),
                field, field, field, field, field, field, field,
                pltpu.VMEM((2, 16, 8, 128), f32), pltpu.VMEM((2, 16, 8, 128), f32),
                pltpu.VMEM((2, 48, 128), f32), pltpu.VMEM((2, 48, 128), f32),
                pltpu.VMEM((8, 32, 128), f32), pltpu.VMEM((8, 32, 128), f32),
                pltpu.VMEM((3, 8, 128), f32), pltpu.VMEM((3, 8, 128), f32),
                pltpu.SemaphoreType.DMA((4,)), pltpu.SemaphoreType.DMA((4,)), pltpu.SemaphoreType.DMA((2, 6)),
            ],
            compiler_params=pltpu.CompilerParams(collective_id=0, has_side_effects=True, vmem_limit_bytes=48 * 1024 * 1024),
            cost_estimate=pl.CostEstimate(flops=10_000_000, bytes_accessed=1_600_000, transcendentals=200_000),
        )(log_range, sea_mask, forcing, cotangent)

    return jax.shard_map(body, mesh=mesh, in_specs=(spec,) * 4, out_specs=(spec, spec), check_vma=False)
```

time: 133 us -> 41.4 us (0.31)
  the two profiles are of different devices: /device:TPU:40 before, /device:TPU:25 now
where the time goes in v1:
time: 41.4 us; the launch traced here: 41.2 us
  Pallas kernels  35.3 us (85%)
  local copies, waits for them, and re-layouts  5.2 us (13%)
  between operations  0.65 us (2%)
    pallas_call x1, Pallas kernels, body(): pl.pallas_call(functools.partial(kernel, sizes), out_shape=[jax.ShapeDtyp...  35.3 us
    unnamed x10, local copies, waits for them, and re-layouts  5.2 us

profile of v1, /device:TPU:25, one launch (start us, length us, event | category | flops | bytes accessed | tf_op | source)
XLA Modules:
  0.0 41.2 jit_solution(8662387212689351158)
XLA Ops:
  0.6 0.0 copy-start
  0.6 0.9 %copy-done = f32[16,32,128]{2,1,0:T(8,128)S(1)} copy-done((f32[16,32,128]{2,1,0:T(8,128)S(1)}, f32[16,32,128]{2,1,0:T(8,128)}, u32[]{:S(2)}) %copy-start) | copy-done | bytes 262168
  1.6 0.0 copy-start.1
  1.6 0.9 %copy-done.1 = s32[16,32,128]{2,1,0:T(8,128)S(1)} copy-done((s32[16,32,128]{2,1,0:T(8,128)S(1)}, s32[16,32,128]{2,1,0:T(8,128)}, u32[]{:S(2)}) %copy-start.1) | copy-done | bytes 262168
  2.5 0.0 copy-start.2
  2.5 0.9 %copy-done.2 = f32[16,32,128]{2,1,0:T(8,128)S(1)} copy-done((f32[16,32,128]{2,1,0:T(8,128)S(1)}, f32[16,32,128]{2,1,0:T(8,128)}, u32[]{:S(2)}) %copy-start.2) | copy-done | bytes 262168
  3.5 0.0 copy-start.3
  3.5 0.9 %copy-done.3 = f32[16,32,128]{2,1,0:T(8,128)S(1)} copy-done((f32[16,32,128]{2,1,0:T(8,128)S(1)}, f32[16,32,128]{2,1,0:T(8,128)}, u32[]{:S(2)}) %copy-start.3) | copy-done | bytes 262168
  4.4 35.3 %shard_map.59 = (f32[16,32,128]{2,1,0:T(8,128)S(1)}, f32[16,32,128]{2,1,0:T(8,128)S(1)}) custom-call(f32[16,32,128]{2,1,0:T(8,128)S(1)} %copy-done, s32[16,32,128]{2,1,0:T(8,128)S(1)} %copy-done.1, f32[16,32,128]{2,1,0:T(8,128)S(1)} %copy-done.2, f32[16,32,128]{2,1,0:T(8,128)S(1)} %copy-done.3), custom_call_target="tpu_custom_call" | custom-call | flops 10000000 | bytes 1600000 | tf_op jit(solution)/shard_map/pallas_call | solution.py:264
  39.8 0.7 %copy.8 = f32[16,32,128]{2,1,0:T(8,128)} copy(f32[16,32,128]{2,1,0:T(8,128)S(1)} %get-tuple-element.4) | data formatting | bytes 524288
  40.5 0.7 %copy.9 = f32[16,32,128]{2,1,0:T(8,128)} copy(f32[16,32,128]{2,1,0:T(8,128)S(1)} %get-tuple-element.5) | data formatting | bytes 524288
Async XLA Ops:
  0.6 1.0 %copy-start = (f32[16,32,128]{2,1,0:T(8,128)S(1)}, f32[16,32,128]{2,1,0:T(8,128)}, u32[]{:S(2)}) copy-start(f32[16,32,128]{2,1,0:T(8,128)} %lr_h.1) | copy-start | bytes 786436
  1.6 0.9 %copy-start.1 = (s32[16,32,128]{2,1,0:T(8,128)S(1)}, s32[16,32,128]{2,1,0:T(8,128)}, u32[]{:S(2)}) copy-start(s32[16,32,128]{2,1,0:T(8,128)} %m_h.1) | copy-start | bytes 786436
  2.5 0.9 %copy-start.2 = (f32[16,32,128]{2,1,0:T(8,128)S(1)}, f32[16,32,128]{2,1,0:T(8,128)}, u32[]{:S(2)}) copy-start(f32[16,32,128]{2,1,0:T(8,128)} %f_h.1) | copy-start | bytes 786436
  3.5 0.9 %copy-start.3 = (f32[16,32,128]{2,1,0:T(8,128)S(1)}, f32[16,32,128]{2,1,0:T(8,128)}, u32[]{:S(2)}) copy-start(f32[16,32,128]{2,1,0:T(8,128)} %c_h.1) | copy-start | bytes 786436

commit v2 on v1

--- a/solution.py
+++ b/solution.py
@@ -10,6 +10,7 @@
 MESH = pl.DeviceIdType.MESH
 RELAX = 0.9
 KEEP = 1.0 - RELAX
+TURNS = (4, 8, 8)
 LAND = RELAX * (1.0 + KEEP + KEEP * KEEP + KEEP * KEEP * KEEP)
 OWN = pl.ds(8, 32)
 
@@ -45,9 +46,9 @@
     return own, n
 
 
-def kernel(sizes, lr_h, m_h, f_h, c_h, it_h, rg_h,
-           lr, ms, fo, co, it, rg, a_, u1, u2, u3, w0, w1, w2,
-           xs, xr, ys, yr, zs, zr, gs, gr, in_sem, out_sem, sem):
+def kernel(sizes, lr_h, m_h, f_h, c_h, it, rg,
+           lr, ms, fo, co, a_, u1, u2, u3, w0, w1, w2,
+           xs, xr, ys, yr, zs, zr, gs, gr, in_sem, sem, ready):
     nx, ny = sizes
     gz, gx, gy = lax.axis_index("gz"), lax.axis_index("gx"), lax.axis_index("gy")
     has = [gx > 0, gx < nx - 1, gy > 0, gy < ny - 1]
@@ -55,7 +56,9 @@
     partner = {"gz": 1 - gz}
 
     barrier = pltpu.get_barrier_semaphore()
-    pl.semaphore_signal(barrier, inc=1, device_id=partner, device_id_type=MESH)
+    @pl.when(gz == 0)
+    def _():
+        pl.semaphore_signal(barrier, inc=1, device_id=partner, device_id_type=MESH)
     for here, device in zip(has, to):
         @pl.when(here)
         def _():
@@ -109,12 +112,24 @@
     for j in range(2):
         zs[6 + j] = a_[16 - j, 0, OWN]
 
-    pl.semaphore_wait(barrier, 1 + sum(h.astype(jnp.int32) for h in has))
+    pl.semaphore_wait(barrier, gz + sum(h.astype(jnp.int32) for h in has))
+
+    @pl.when(gz == 1)
+    def _():
+        pl.semaphore_signal(ready, inc=1, device_id=partner, device_id_type=MESH)
+
+    turn = sum((gx * 8 // nx >= at).astype(jnp.int32) for at in TURNS)
+
+    def send_layers(phase):
+        @pl.when((gz == 1) & (turn == phase))
+        def _():
+            zcopy.start()
+
     for here, copy in zip(has[:2], xcopy):
         @pl.when(here)
         def _():
             copy.start()
-    zcopy.start()
+    send_layers(0)
 
     for here, copy in zip((has[1], has[0]), xcopy):
         @pl.when(here)
@@ -145,6 +160,7 @@
         @pl.when(here)
         def _():
             copy.start()
+    send_layers(1)
     for here, copy in zip((has[3], has[2]), ycopy):
         @pl.when(here)
         def _():
@@ -179,6 +195,13 @@
             at += 2 * depth
         columns = part if columns is None else jnp.where(lane8 >= 16 * k, part, columns)
     gs[0], gs[1], gs[2] = top, low, columns
+    send_layers(2)
+
+    @pl.when(gz == 0)
+    def _():
+        pl.semaphore_wait(ready, 1)
+        zcopy.start()
+
     gcopy.start()
     lax.fori_loop(3, 16, y_halo, carry)
 
@@ -209,14 +232,9 @@
     first = sweep(u1, u2, w0, w1)
     second = sweep(u2, u3, w1, w2)
     lax.fori_loop(1, 16, first, 0)
+    send_layers(3)
     lax.fori_loop(1, 15, second, 0)
     lax.fori_loop(1, 14, finish, 0)
-
-    bulk, edge = pl.ds(3 * gz, 13), pl.ds(13 * (1 - gz), 3)
-    stores = [pltpu.make_async_copy(v.at[part], h.at[part], out_sem.at[i])
-              for i, (v, h, part) in enumerate(((it, it_h, bulk), (rg, rg_h, bulk), (it, it_h, edge), (rg, rg_h, edge)))]
-    stores[0].start()
-    stores[1].start()
 
     zcopy.wait_recv()
     for j in range(3):
@@ -240,8 +258,6 @@
     lax.fori_loop(16, 19, first, 0)
     lax.fori_loop(15, 18, second, 0)
     lax.fori_loop(14, 17, finish, 0)
-    stores[2].start()
-    stores[3].start()
 
     for here, copy in zip(has, xcopy + ycopy):
         @pl.when(here)
@@ -249,8 +265,6 @@
             copy.wait_send()
     zcopy.wait_send()
     gcopy.wait_send()
-    for store in stores:
-        store.wait()
 
 
 def solution(mesh):
@@ -263,21 +277,21 @@
         field = pltpu.VMEM((20, 2, 48, 128), f32)
         return pl.pallas_call(
             functools.partial(kernel, sizes),
-            out_shape=[jax.ShapeDtypeStruct(block, f32)] * 2,
-            in_specs=[pl.BlockSpec(memory_space=pl.ANY)] * 4,
-            out_specs=[pl.BlockSpec(memory_space=pl.ANY)] * 2,
+            out_shape=[pltpu.VMEM(block, f32)] * 2,
+            in_specs=[pl.BlockSpec(memory_space=pltpu.HBM)] * 4,
+            out_specs=[pl.BlockSpec(memory_space=pltpu.VMEM)] * 2,
             scratch_shapes=[
                 pltpu.VMEM(block, f32), pltpu.VMEM(block, jnp.int32), pltpu.VMEM(block, f32), pltpu.VMEM(block, f32),
-                pltpu.VMEM(block, f32), pltpu.VMEM(block, f32),
                 field, field, field, field, field, field, field,
                 pltpu.VMEM((2, 16, 8, 128), f32), pltpu.VMEM((2, 16, 8, 128), f32),
                 pltpu.VMEM((2, 48, 128), f32), pltpu.VMEM((2, 48, 128), f32),
                 pltpu.VMEM((8, 32, 128), f32), pltpu.VMEM((8, 32, 128), f32),
                 pltpu.VMEM((3, 8, 128), f32), pltpu.VMEM((3, 8, 128), f32),
-                pltpu.SemaphoreType.DMA((4,)), pltpu.SemaphoreType.DMA((4,)), pltpu.SemaphoreType.DMA((2, 6)),
+                pltpu.SemaphoreType.DMA((4,)), pltpu.SemaphoreType.DMA((2, 6)),
+                pltpu.SemaphoreType.REGULAR,
             ],
             compiler_params=pltpu.CompilerParams(collective_id=0, has_side_effects=True, vmem_limit_bytes=48 * 1024 * 1024),
             cost_estimate=pl.CostEstimate(flops=10_000_000, bytes_accessed=1_600_000, transcendentals=200_000),
-        )(log_range, sea_mask, forcing, cotangent)
+        )(*(pltpu.with_memory_space_constraint(x, pltpu.HBM) for x in (log_range, sea_mask, forcing, cotangent)))
 
     return jax.shard_map(body, mesh=mesh, in_specs=(spec,) * 4, out_specs=(spec, spec), check_vma=False)

time: 41.4 us -> 33.4 us (0.81)
  Pallas kernels: 35.3 us -> 31.2 us
  local copies, waits for them, and re-layouts: 5.2 us -> 1.41 us
    pallas_call x1, Pallas kernels: 35.3 us -> 31.2 us  [body(): pl.pallas_call(functools.partial(kernel, sizes), out_shape=[pltpu.VMEM(bl...]
    unnamed x10 -> x2, local copies, waits for them, and re-layouts: 5.2 us -> 1.41 us
where the time goes in v2:
time: 33.4 us; the launch traced here: 33.2 us
  Pallas kernels  31.2 us (93%)
  local copies, waits for them, and re-layouts  1.41 us (4%)
  between operations  0.64 us (2%)
    pallas_call x1, Pallas kernels, body(): pl.pallas_call(functools.partial(kernel, sizes), out_shape=[pltpu.VMEM(bl...  31.2 us
    unnamed x2, local copies, waits for them, and re-layouts  1.41 us

profile of v2, /device:TPU:25, one launch (start us, length us, event | category | flops | bytes accessed | tf_op | source)
XLA Modules:
  0.0 33.2 jit_solution(16426768257643380910)
XLA Ops:
  0.6 31.2 %shard_map.59 = (f32[16,32,128]{2,1,0:T(8,128)S(1)}, f32[16,32,128]{2,1,0:T(8,128)S(1)}) custom-call(f32[16,32,128]{2,1,0:T(8,128)} %lr_h.1, s32[16,32,128]{2,1,0:T(8,128)} %m_h.1, f32[16,32,128]{2,1,0:T(8,128)} %f_h.1, f32[16,32,128]{2,1,0:T(8,128)} %c_h.1), custom_call_target="tpu_custom_call" | custom-call | flops 10000000 | bytes 1600000 | tf_op jit(solution)/shard_map/pallas_call | solution.py:278
  31.8 0.7 %copy.8 = f32[16,32,128]{2,1,0:T(8,128)} copy(f32[16,32,128]{2,1,0:T(8,128)S(1)} %get-tuple-element.2) | data formatting | bytes 524288
  32.5 0.7 %copy.9 = f32[16,32,128]{2,1,0:T(8,128)} copy(f32[16,32,128]{2,1,0:T(8,128)S(1)} %get-tuple-element.3) | data formatting | bytes 524288

commit v3 on v2

v3 whole, which is shorter than its diff:
```python
import functools

import jax
import jax.numpy as jnp
from jax import lax
from jax.experimental import pallas as pl
from jax.experimental.pallas import tpu as pltpu
from jax.sharding import PartitionSpec as P

MESH = pl.DeviceIdType.MESH
SIDES = ((-1, 0), (1, 0), (0, -1), (0, 1), (-1, -1), (1, -1), (-1, 1), (1, 1))
RELAX = 0.9
KEEP = 1.0 - RELAX
TURNS = (0, 0, 0, 0, 0, 1, 2, 2)
LAND = RELAX * (1.0 + KEEP + KEEP * KEEP + KEEP * KEEP * KEEP)
OWN = pl.ds(8, 32)


def roll(value, shift, axis):
    size = value.shape[axis]
    shift = shift % size
    return pltpu.roll(value, shift, axis) if shift else value


def stencil_full(ref, i):
    lane = lax.broadcasted_iota(jnp.int32, (48, 128), 1)
    first, last = lane == 0, lane == 127
    c0, c1 = ref[i, 0], ref[i, 1]
    r0, r1 = roll(c0, 1, 1), roll(c1, 1, 1)
    l0, l1 = roll(c0, -1, 1), roll(c1, -1, 1)
    n0 = ref[i - 1, 0] + ref[i + 1, 0] + (roll(c0, 1, 0) + roll(c0, -1, 0))
    n1 = ref[i - 1, 1] + ref[i + 1, 1] + (roll(c1, 1, 0) + roll(c1, -1, 0))
    n0 = n0 + jnp.where(first, r1, r0) + jnp.where(last, l1, l0)
    n1 = n1 + jnp.where(first, r0, r1) + jnp.where(last, l0, l1)
    return (c0, c1), (n0, n1)


def stencil_own(ref, i):
    lane = lax.broadcasted_iota(jnp.int32, (32, 128), 1)
    c = ref[i, 0]
    own = c[8:40]
    side = ref[i, 1, OWN]
    n = ref[i - 1, 0, OWN] + ref[i + 1, 0, OWN]
    n = n + (roll(c, 1, 0)[8:40] + roll(c, -1, 0)[8:40])
    n = n + jnp.where(lane == 0, roll(side, 1, 1), roll(own, 1, 1))
    n = n + jnp.where(lane == 127, roll(side, -1, 1), roll(own, -1, 1))
    return own, n


def kernel(sizes, lr_h, m_h, f_h, c_h, it, rg,
           lr, ms, fo, co, a_, u1, u2, u3, w0, w1, w2,
           xs, xr, ys, yr, zs, zr, gs, gr, in_sem, sem, ready):
    nx, ny = sizes
    gz, gx, gy = lax.axis_index("gz"), lax.axis_index("gx"), lax.axis_index("gy")
    partner = {"gz": 1 - gz}
    has = {}
    for x, y in SIDES:
        here = []
        if x:
            here.append(gx > 0 if x < 0 else gx < nx - 1)
        if y:
            here.append(gy > 0 if y < 0 else gy < ny - 1)
        has[x, y] = here[0] if len(here) == 1 else here[0] & here[1]

    def at(side):
        return {"gx": gx + side[0], "gy": gy + side[1]}

    barrier = pltpu.get_barrier_semaphore()

    @pl.when(gz == 0)
    def _():
        pl.semaphore_signal(barrier, inc=1, device_id=partner, device_id_type=MESH)

    for side in SIDES:
        @pl.when(has[side])
        def _():
            pl.semaphore_signal(barrier, inc=1, device_id=at(side), device_id_type=MESH)

    loads = [pltpu.make_async_copy(h, v, in_sem.at[i]) for i, (h, v) in enumerate(((lr_h, lr), (m_h, ms), (f_h, fo), (c_h, co)))]
    for load in loads:
        load.start()

    def remote(src, dst, i, device):
        return pltpu.make_async_remote_copy(src_ref=src, dst_ref=dst, send_sem=sem.at[0, i], recv_sem=sem.at[1, i],
                                            device_id=device, device_id_type=MESH)

    low, mid, top = pl.ds(40, 8), pl.ds(8, 32), pl.ds(0, 8)
    first8, last8 = pl.ds(0, 8), pl.ds(24, 8)
    copies = {}
    for i, (side, src, dst) in enumerate((
        ((-1, 0), xs.at[0], xr.at[0]), ((1, 0), xs.at[1], xr.at[1]),
        ((0, -1), ys.at[0], yr.at[0, mid]), ((0, 1), ys.at[1], yr.at[1, mid]),
        ((-1, -1), ys.at[0, first8], yr.at[0, low]), ((1, -1), ys.at[0, last8], yr.at[0, top]),
        ((-1, 1), ys.at[1, first8], yr.at[1, low]), ((1, 1), ys.at[1, last8], yr.at[1, top]),
    )):
        copies[side] = remote(src, dst, i, at(side))
    zcopy = remote(zs, zr, 8, partner)
    gcopy = remote(gs, gr, 9, partner)

    def source(i):
        return jnp.where(gz == 0, i, 15 - i)

    row8 = lax.broadcasted_iota(jnp.int32, (8, 128), 0)
    lane8 = lax.broadcasted_iota(jnp.int32, (8, 128), 1)
    lane32 = lax.broadcasted_iota(jnp.int32, (32, 128), 1)
    lane48 = lax.broadcasted_iota(jnp.int32, (48, 128), 1)
    zero = jnp.zeros((48, 128), jnp.float32)
    for ref in (u1, u2, u3, w0, w1, w2):
        ref[0, 0] = zero
        ref[0, 1] = zero
    for load in loads:
        load.wait()

    def prepare(i, carry):
        left, right = carry
        z = source(i)
        mask = ms[z].astype(jnp.float32)
        inverse = 1.0 / (mask * (6.0 + jnp.exp(-2.0 * lr[z])) + (1.0 - mask))
        weight = RELAX * mask * inverse
        u, w = weight * fo[z], weight * co[z]
        a_[i + 1, 0, OWN] = weight
        u1[i + 1, 0, OWN] = u
        w0[i + 1, 0, OWN] = w
        up_u, up_w, up_a = u[:8], w[:8], weight[:8]
        dn_u, dn_w, dn_a = u[24:], w[24:], weight[24:]
        xs[0, i] = jnp.where(row8 < 3, up_u, jnp.where(row8 < 6, roll(up_w, 3, 0), roll(up_a, 6, 0)))
        xs[1, i] = jnp.where(row8 >= 5, dn_u, jnp.where(row8 >= 2, roll(dn_w, -3, 0), roll(dn_a, -6, 0)))
        to_right = jnp.where(lane32 < 3, roll(u, 3, 1), jnp.where(lane32 < 6, roll(w, 6, 1), roll(weight, 8, 1)))
        to_left = jnp.where(lane32 < 3, u, jnp.where(lane32 < 6, roll(w, 3, 1), roll(weight, 6, 1)))
        left = jnp.where(lane32 < 8, to_left, roll(left, 8, 1))
        right = jnp.where(lane32 < 8, to_right, roll(right, 8, 1))
        return left, right

    left, right = lax.fori_loop(0, 16, prepare, (zero[:32], zero[:32]))
    ys[0] = left
    ys[1] = right
    for j, (ref, i) in enumerate(((u1, 16), (u1, 15), (w0, 16), (w0, 15), (a_, 16))):
        zs[j] = ref[i, 0, OWN]

    pl.semaphore_wait(barrier, gz + sum(h.astype(jnp.int32) for h in has.values()))

    @pl.when(gz == 1)
    def _():
        pl.semaphore_signal(ready, inc=1, device_id=partner, device_id_type=MESH)

    place = gx * 8 // nx
    turn = sum(jnp.where(place == i, t, 0) for i, t in enumerate(TURNS) if t)

    def send_layers(phase):
        @pl.when((gz == 1) & (turn == phase))
        def _():
            zcopy.start()
            if phase > 1:
                gcopy.start()

    for side in SIDES:
        @pl.when(has[side])
        def _():
            copies[side].start()
    send_layers(0)

    for side in SIDES:
        @pl.when(has[-side[0], -side[1]])
        def _():
            copies[side].wait_recv()
    send_layers(1)

    def halo(j, carry):
        left, right = carry
        i = 16 - j
        below = jnp.where(has[1, 0], xr[0, i - 1], 0.0)
        above = jnp.where(has[-1, 0], xr[1, i - 1], 0.0)
        u1[i, 0, low] = below
        w0[i, 0, low] = roll(below, -3, 0)
        a_[i, 0, low] = roll(below, -6, 0)
        u1[i, 0, top] = above
        w0[i, 0, top] = roll(above, 3, 0)
        a_[i, 0, top] = roll(above, 6, 0)
        half = lane48 < 64
        u1[i, 1] = jnp.where(half, right, roll(left, -3, 1))
        w0[i, 1] = jnp.where(half, roll(right, -3, 1), roll(left, -6, 1))
        a_[i, 1] = jnp.where(half, roll(right, -6, 1), roll(left, -8, 1))
        return roll(left, -8, 1), roll(right, -8, 1)

    def arrived(slot, y):
        parts = [jnp.where(has[x, y], yr[slot, rows], 0.0) for x, rows in ((-1, top), (0, mid), (1, low))]
        return jnp.concatenate(parts, axis=0)

    carry = lax.fori_loop(0, 3, halo, (arrived(1, -1), arrived(0, 1)))

    def sweep(old_u, new_u, old_w, new_w):
        def run(i, _):
            (c0, c1), (n0, n1) = stencil_full(old_u, i)
            new_u[i, 0] = KEEP * c0 + u1[i, 0] + a_[i, 0] * n0
            new_u[i, 1] = KEEP * c1 + u1[i, 1] + a_[i, 1] * n1
            (c0, c1), (n0, n1) = stencil_full(old_w, i)
            new_w[i, 0] = KEEP * c0 + a_[i, 0] * n0
            new_w[i, 1] = KEEP * c1 + a_[i, 1] * n1
            return 0
        return run

    def finish(i, _):
        z = source(i - 1)
        weight, s1 = a_[i, 0, OWN], u1[i, 0, OWN]
        c, n = stencil_own(u3, i)
        s4 = s1 + weight * n
        b, n = stencil_own(w2, i)
        w3 = KEEP * b + weight * n
        second = u2[i, 0, OWN]
        total = w0[i, 0, OWN] * s4 + w1[i, 0, OWN] * (c - KEEP * second) + b * (second - KEEP * s1) + w3 * s1
        rg[z] = (2.0 / RELAX) * jnp.exp(-2.0 * lr[z]) * total
        it[z] = jnp.where(ms[z] > 0, KEEP * c + s4, LAND * fo[z])
        return 0

    first = sweep(u1, u2, w0, w1)
    second = sweep(u2, u3, w1, w2)
    first(15, 0)
    ring = ((u1, 16, 2), (w0, 16, 2), (u1, 15, 1), (w0, 15, 1), (a_, 16, 1))
    above, below, columns = None, None, None
    at = 0
    for ref, i, depth in ring:
        t = roll(ref[i, 0, top], -at, 0)
        b = roll(ref[i, 0, low], at, 0)
        above = t if above is None else jnp.where(row8 < 8 - at, t, above)
        below = b if below is None else jnp.where(row8 >= at, b, below)
        at += depth
    for k in range(6):
        part, at = None, 0
        for ref, i, depth in ring:
            c = roll(ref[i, 1, pl.ds(8 * k, 8)], at + depth + 16 * k, 1)
            part = c if part is None else jnp.where(lane8 >= at + 16 * k, c, part)
            at += 2 * depth
        columns = part if columns is None else jnp.where(lane8 >= 16 * k, part, columns)
    gs[first8] = above
    gs[pl.ds(8, 8)] = below
    gs[pl.ds(16, 8)] = columns
    gs[pl.ds(24, 32)] = u2[15, 0, OWN]
    gs[pl.ds(56, 32)] = w1[15, 0, OWN]
    @pl.when((gz == 1) & (turn < 2))
    def _():
        gcopy.start()

    send_layers(2)

    lax.fori_loop(3, 16, halo, carry)
    send_layers(3)
    lax.fori_loop(1, 6, first, 0)
    send_layers(4)
    lax.fori_loop(6, 15, first, 0)

    @pl.when(gz == 0)
    def _():
        pl.semaphore_wait(ready, 1)
        zcopy.start()
        gcopy.start()

    lax.fori_loop(1, 15, second, 0)
    lax.fori_loop(1, 14, finish, 0)

    zcopy.wait_recv()
    for j, (ref, i) in enumerate(((u1, 17), (u1, 18), (w0, 17), (w0, 18), (a_, 17))):
        ref[i, 0, OWN] = zr[j]
    gcopy.wait_recv()
    above, below, columns = gr[first8], gr[pl.ds(8, 8)], gr[pl.ds(16, 8)]
    u2[18, 0, OWN] = gr[pl.ds(24, 32)]
    w1[18, 0, OWN] = gr[pl.ds(56, 32)]
    at = 0
    for ref, i, depth in ring:
        ref[33 - i, 0, top] = roll(above, at, 0)
        ref[33 - i, 0, low] = roll(below, -at, 0)
        at += depth
    for k in range(6):
        at = 0
        for ref, i, depth in ring:
            ref[33 - i, 1, pl.ds(8 * k, 8)] = roll(columns, -(at + depth + 16 * k), 1)
            at += 2 * depth

    lax.fori_loop(16, 18, first, 0)
    lax.fori_loop(15, 18, second, 0)
    lax.fori_loop(14, 17, finish, 0)

    for side in SIDES:
        @pl.when(has[side])
        def _():
            copies[side].wait_send()
    zcopy.wait_send()
    gcopy.wait_send()


def solution(mesh):
    sizes = mesh.shape["gx"], mesh.shape["gy"]
    spec = P("gz", "gx", "gy")

    def body(log_range, sea_mask, forcing, cotangent):
        block = log_range.shape
        f32 = jnp.float32
        field = pltpu.VMEM((19, 2, 48, 128), f32)
        return pl.pallas_call(
            functools.partial(kernel, sizes),
            out_shape=[pltpu.VMEM(block, f32)] * 2,
            in_specs=[pl.BlockSpec(memory_space=pltpu.HBM)] * 4,
            out_specs=[pl.BlockSpec(memory_space=pltpu.VMEM)] * 2,
            scratch_shapes=[
                pltpu.VMEM(block, f32), pltpu.VMEM(block, jnp.int32), pltpu.VMEM(block, f32), pltpu.VMEM(block, f32),
                field, field, field, field, field, field, field,
                pltpu.VMEM((2, 16, 8, 128), f32), pltpu.VMEM((2, 16, 8, 128), f32),
                pltpu.VMEM((2, 32, 128), f32), pltpu.VMEM((2, 48, 128), f32),
                pltpu.VMEM((5, 32, 128), f32), pltpu.VMEM((5, 32, 128), f32),
                pltpu.VMEM((88, 128), f32), pltpu.VMEM((88, 128), f32),
                pltpu.SemaphoreType.DMA((4,)), pltpu.SemaphoreType.DMA((2, 10)),
                pltpu.SemaphoreType.REGULAR,
            ],
            compiler_params=pltpu.CompilerParams(collective_id=0, has_side_effects=True, vmem_limit_bytes=48 * 1024 * 1024),
            cost_estimate=pl.CostEstimate(flops=10_000_000, bytes_accessed=1_600_000, transcendentals=200_000),
        )(*(pltpu.with_memory_space_constraint(x, pltpu.HBM) for x in (log_range, sea_mask, forcing, cotangent)))

    def store(it, rg, it_h, rg_h, sem):
        copies = [pltpu.make_async_copy(v.at[pl.ds(16 * h, 16)], o.at[pl.ds(16 * h, 16)], sem.at[i, h])
                  for i, (v, o) in enumerate(((it, it_h), (rg, rg_h))) for h in range(1)]
        for copy in copies:
            copy.start()
        for copy in copies:
            copy.wait()

    def whole(*args):
        parts = body(*args)
        parts = [pltpu.with_memory_space_constraint(x, pltpu.VMEM) for x in parts]
        return pl.pallas_call(store, out_shape=[jax.ShapeDtypeStruct(x.shape, jnp.float32) for x in parts],
                              in_specs=[pl.BlockSpec(memory_space=pltpu.VMEM)] * 2,
                              out_specs=[pl.BlockSpec(memory_space=pl.ANY)] * 2,
                              scratch_shapes=[pltpu.SemaphoreType.DMA((2, 1))])(*parts)

    return jax.shard_map(whole, mesh=mesh, in_specs=(spec,) * 4, out_specs=(spec, spec), check_vma=False)
```

time: 33.4 us -> 31.5 us (0.943)
  the two profiles are of different devices: /device:TPU:25 before, /device:TPU:57 now
where the time goes in v3:
time: 31.5 us; the launch traced here: 31.4 us
  Pallas kernels  30.7 us (97%)
  between operations  0.64 us (2%)
    pallas_call x1, Pallas kernels, body(): pl.pallas_call(functools.partial(kernel, sizes), out_shape=[pltpu.VMEM(bl...  29.9 us
    pallas_call x1, Pallas kernels, whole(): pl.pallas_call(store, out_shape=[jax.ShapeDtypeStruct(x.shape, jnp.float3...  0.81 us

profile of v3, /device:TPU:57, one launch (start us, length us, event | category | flops | bytes accessed | tf_op | source)
XLA Modules:
  0.0 31.4 jit_solution(2500439113502043056)
XLA Ops:
  0.6 29.9 %shard_map.59 = (f32[16,32,128]{2,1,0:T(8,128)S(1)}, f32[16,32,128]{2,1,0:T(8,128)S(1)}) custom-call(f32[16,32,128]{2,1,0:T(8,128)} %lr_h.1, s32[16,32,128]{2,1,0:T(8,128)} %m_h.1, f32[16,32,128]{2,1,0:T(8,128)} %f_h.1, f32[16,32,128]{2,1,0:T(8,128)} %c_h.1), custom_call_target="tpu_custom_call" | custom-call | flops 10000000 | bytes 1600000 | tf_op jit(solution)/shard_map/pallas_call | solution.py:298
  30.6 0.8 %shard_map.60 = (f32[16,32,128]{2,1,0:T(8,128)}, f32[16,32,128]{2,1,0:T(8,128)}) custom-call(f32[16,32,128]{2,1,0:T(8,128)S(1)} %get-tuple-element.4.it, f32[16,32,128]{2,1,0:T(8,128)S(1)} %get-tuple-element.5.rg), custom_call_target="tpu_custom_call" | custom-call | tf_op jit(solution)/shard_map/pallas_call | solution.py:328

commit v4 on v3

--- a/solution.py
+++ b/solution.py
@@ -11,7 +11,7 @@
 SIDES = ((-1, 0), (1, 0), (0, -1), (0, 1), (-1, -1), (1, -1), (-1, 1), (1, 1))
 RELAX = 0.9
 KEEP = 1.0 - RELAX
-TURNS = (0, 0, 0, 0, 0, 1, 2, 2)
+TURNS = (0, 0, 0, 0, 0, 2, 2, 2)
 LAND = RELAX * (1.0 + KEEP + KEEP * KEEP + KEEP * KEEP * KEEP)
 OWN = pl.ds(8, 32)
 
@@ -86,14 +86,16 @@
 
     low, mid, top = pl.ds(40, 8), pl.ds(8, 32), pl.ds(0, 8)
     first8, last8 = pl.ds(0, 8), pl.ds(24, 8)
+    near, rest = pl.ds(13, 3), pl.ds(0, 13)
     copies = {}
     for i, (side, src, dst) in enumerate((
-        ((-1, 0), xs.at[0], xr.at[0]), ((1, 0), xs.at[1], xr.at[1]),
+        ((-1, 0), xs.at[0, near], xr.at[0, near]), ((1, 0), xs.at[1, near], xr.at[1, near]),
         ((0, -1), ys.at[0], yr.at[0, mid]), ((0, 1), ys.at[1], yr.at[1, mid]),
         ((-1, -1), ys.at[0, first8], yr.at[0, low]), ((1, -1), ys.at[0, last8], yr.at[0, top]),
         ((-1, 1), ys.at[1, first8], yr.at[1, low]), ((1, 1), ys.at[1, last8], yr.at[1, top]),
     )):
         copies[side] = remote(src, dst, i, at(side))
+    far = {side: remote(xs.at[i, rest], xr.at[i, rest], 10 + i, at(side)) for i, side in enumerate(SIDES[:2])}
     zcopy = remote(zs, zr, 8, partner)
     gcopy = remote(gs, gr, 9, partner)
 
@@ -158,6 +160,10 @@
         def _():
             copies[side].start()
     send_layers(0)
+    for side in far:
+        @pl.when(has[side])
+        def _():
+            far[side].start()
 
     for side in SIDES:
         @pl.when(has[-side[0], -side[1]])
@@ -242,6 +248,10 @@
 
     send_layers(2)
 
+    for side in far:
+        @pl.when(has[-side[0], -side[1]])
+        def _():
+            far[side].wait_recv()
     lax.fori_loop(3, 16, halo, carry)
     send_layers(3)
     lax.fori_loop(1, 6, first, 0)
@@ -283,6 +293,10 @@
         @pl.when(has[side])
         def _():
             copies[side].wait_send()
+    for side in far:
+        @pl.when(has[side])
+        def _():
+            far[side].wait_send()
     zcopy.wait_send()
     gcopy.wait_send()
 
@@ -307,7 +321,7 @@
                 pltpu.VMEM((2, 32, 128), f32), pltpu.VMEM((2, 48, 128), f32),
                 pltpu.VMEM((5, 32, 128), f32), pltpu.VMEM((5, 32, 128), f32),
                 pltpu.VMEM((88, 128), f32), pltpu.VMEM((88, 128), f32),
-                pltpu.SemaphoreType.DMA((4,)), pltpu.SemaphoreType.DMA((2, 10)),
+                pltpu.SemaphoreType.DMA((4,)), pltpu.SemaphoreType.DMA((2, 12)),
                 pltpu.SemaphoreType.REGULAR,
             ],
             compiler_params=pltpu.CompilerParams(collective_id=0, has_side_effects=True, vmem_limit_bytes=48 * 1024 * 1024),

time: 31.5 us -> 31.4 us (level)
  the two profiles are of different devices: /device:TPU:57 before, /device:TPU:248 now
where the time goes in v4:
time: 31.4 us; the launch traced here: 31.2 us
  Pallas kernels  30.6 us (97%)
  between operations  0.64 us (2%)
    pallas_call x1, Pallas kernels, body(): pl.pallas_call(functools.partial(kernel, sizes), out_shape=[pltpu.VMEM(bl...  29.8 us
    pallas_call x1, Pallas kernels, whole(): pl.pallas_call(store, out_shape=[jax.ShapeDtypeStruct(x.shape, jnp.float3...  0.81 us

profile of v4, /device:TPU:248, one launch (start us, length us, event | category | flops | bytes accessed | tf_op | source)
XLA Modules:
  0.0 31.2 jit_solution(13238454000305623803)
XLA Ops:
  0.6 29.8 %shard_map.59 = (f32[16,32,128]{2,1,0:T(8,128)S(1)}, f32[16,32,128]{2,1,0:T(8,128)S(1)}) custom-call(f32[16,32,128]{2,1,0:T(8,128)} %lr_h.1, s32[16,32,128]{2,1,0:T(8,128)} %m_h.1, f32[16,32,128]{2,1,0:T(8,128)} %f_h.1, f32[16,32,128]{2,1,0:T(8,128)} %c_h.1), custom_call_target="tpu_custom_call" | custom-call | flops 10000000 | bytes 1600000 | tf_op jit(solution)/shard_map/pallas_call | solution.py:312
  30.4 0.8 %shard_map.60 = (f32[16,32,128]{2,1,0:T(8,128)}, f32[16,32,128]{2,1,0:T(8,128)}) custom-call(f32[16,32,128]{2,1,0:T(8,128)S(1)} %get-tuple-element.4.it, f32[16,32,128]{2,1,0:T(8,128)S(1)} %get-tuple-element.5.rg), custom_call_target="tpu_custom_call" | custom-call | tf_op jit(solution)/shard_map/pallas_call | solution.py:342

commit v5 on v4

--- a/solution.py
+++ b/solution.py
@@ -8,10 +8,10 @@
 from jax.sharding import PartitionSpec as P
 
 MESH = pl.DeviceIdType.MESH
-SIDES = ((-1, 0), (1, 0), (0, -1), (0, 1), (-1, -1), (1, -1), (-1, 1), (1, 1))
+SIDES = ((-1, -1), (1, -1), (-1, 1), (1, 1), (0, -1), (0, 1), (-1, 0), (1, 0))
 RELAX = 0.9
 KEEP = 1.0 - RELAX
-TURNS = (0, 0, 0, 0, 0, 2, 2, 2)
+TURNS = (0, 0, 0, 0, 0, 3, 2, 2)
 LAND = RELAX * (1.0 + KEEP + KEEP * KEEP + KEEP * KEEP * KEEP)
 OWN = pl.ds(8, 32)
 
@@ -95,7 +95,7 @@
         ((-1, 1), ys.at[1, first8], yr.at[1, low]), ((1, 1), ys.at[1, last8], yr.at[1, top]),
     )):
         copies[side] = remote(src, dst, i, at(side))
-    far = {side: remote(xs.at[i, rest], xr.at[i, rest], 10 + i, at(side)) for i, side in enumerate(SIDES[:2])}
+    far = {side: remote(xs.at[i, rest], xr.at[i, rest], 10 + i, at(side)) for i, side in enumerate(SIDES[6:])}
     zcopy = remote(zs, zr, 8, partner)
     gcopy = remote(gs, gr, 9, partner)
 
@@ -133,7 +133,7 @@
         right = jnp.where(lane32 < 8, to_right, roll(right, 8, 1))
         return left, right
 
-    left, right = lax.fori_loop(0, 16, prepare, (zero[:32], zero[:32]))
+    left, right = lax.fori_loop(0, 16, prepare, (zero[:32], zero[:32]), unroll=2)
     ys[0] = left
     ys[1] = right
     for j, (ref, i) in enumerate(((u1, 16), (u1, 15), (w0, 16), (w0, 15), (a_, 16))):
@@ -192,7 +192,7 @@
         parts = [jnp.where(has[x, y], yr[slot, rows], 0.0) for x, rows in ((-1, top), (0, mid), (1, low))]
         return jnp.concatenate(parts, axis=0)
 
-    carry = lax.fori_loop(0, 3, halo, (arrived(1, -1), arrived(0, 1)))
+    carry = lax.fori_loop(0, 3, halo, (arrived(1, -1), arrived(0, 1)), unroll=True)
 
     def sweep(old_u, new_u, old_w, new_w):
         def run(i, _):
@@ -252,19 +252,18 @@
         @pl.when(has[-side[0], -side[1]])
         def _():
             far[side].wait_recv()
+    send_layers(3)
     lax.fori_loop(3, 16, halo, carry)
-    send_layers(3)
-    lax.fori_loop(1, 6, first, 0)
+    lax.fori_loop(1, 6, first, 0, unroll=5)
     send_layers(4)
-    lax.fori_loop(6, 15, first, 0)
-
+    lax.fori_loop(6, 15, first, 0, unroll=3)
+
+    lax.fori_loop(1, 15, second, 0, unroll=2)
     @pl.when(gz == 0)
     def _():
         pl.semaphore_wait(ready, 1)
         zcopy.start()
         gcopy.start()
-
-    lax.fori_loop(1, 15, second, 0)
     lax.fori_loop(1, 14, finish, 0)
 
     zcopy.wait_recv()
@@ -285,9 +284,9 @@
             ref[33 - i, 1, pl.ds(8 * k, 8)] = roll(columns, -(at + depth + 16 * k), 1)
             at += 2 * depth
 
-    lax.fori_loop(16, 18, first, 0)
-    lax.fori_loop(15, 18, second, 0)
-    lax.fori_loop(14, 17, finish, 0)
+    lax.fori_loop(16, 18, first, 0, unroll=True)
+    lax.fori_loop(15, 18, second, 0, unroll=True)
+    lax.fori_loop(14, 17, finish, 0, unroll=True)
 
     for side in SIDES:
         @pl.when(has[side])

time: 31.4 us -> 30.7 us (0.978)
  the two profiles are of different devices: /device:TPU:248 before, /device:TPU:56 now
where the time goes in v5:
time: 30.7 us; the launch traced here: 30.6 us
  Pallas kernels  30 us (98%)
  between operations  0.64 us (2%)
    pallas_call x1, Pallas kernels, body(): pl.pallas_call(functools.partial(kernel, sizes), out_shape=[pltpu.VMEM(bl...  29.2 us
    pallas_call x1, Pallas kernels, whole(): pl.pallas_call(store, out_shape=[jax.ShapeDtypeStruct(x.shape, jnp.float3...  0.81 us

profile of v5, /device:TPU:56, one launch (start us, length us, event | category | flops | bytes accessed | tf_op | source)
XLA Modules:
  0.0 30.6 jit_solution(14645838978976519948)
XLA Ops:
  0.6 29.2 %shard_map.59 = (f32[16,32,128]{2,1,0:T(8,128)S(1)}, f32[16,32,128]{2,1,0:T(8,128)S(1)}) custom-call(f32[16,32,128]{2,1,0:T(8,128)} %lr_h.1, s32[16,32,128]{2,1,0:T(8,128)} %m_h.1, f32[16,32,128]{2,1,0:T(8,128)} %f_h.1, f32[16,32,128]{2,1,0:T(8,128)} %c_h.1), custom_call_target="tpu_custom_call" | custom-call | flops 10000000 | bytes 1600000 | tf_op jit(solution)/shard_map/pallas_call | solution.py:311
  29.8 0.8 %shard_map.60 = (f32[16,32,128]{2,1,0:T(8,128)}, f32[16,32,128]{2,1,0:T(8,128)}) custom-call(f32[16,32,128]{2,1,0:T(8,128)S(1)} %get-tuple-element.4.it, f32[16,32,128]{2,1,0:T(8,128)S(1)} %get-tuple-element.5.rg), custom_call_target="tpu_custom_call" | custom-call | tf_op jit(solution)/shard_map/pallas_call | solution.py:341

commit v6 on v5

--- a/solution.py
+++ b/solution.py
@@ -47,9 +47,20 @@
     return own, n
 
 
+def last_step(i, z, lr, ms, fo, a_, u1, u2, u3, w0, w1, w2):
+    weight, s1 = a_[i, 0, OWN], u1[i, 0, OWN]
+    c, n = stencil_own(u3, i)
+    s4 = s1 + weight * n
+    b, n = stencil_own(w2, i)
+    w3 = KEEP * b + weight * n
+    second = u2[i, 0, OWN]
+    total = w0[i, 0, OWN] * s4 + w1[i, 0, OWN] * (c - KEEP * second) + b * (second - KEEP * s1) + w3 * s1
+    return jnp.where(ms[z] > 0, KEEP * c + s4, LAND * fo[z]), (2.0 / RELAX) * jnp.exp(-2.0 * lr[z]) * total
+
+
 def kernel(sizes, lr_h, m_h, f_h, c_h, it, rg,
-           lr, ms, fo, co, a_, u1, u2, u3, w0, w1, w2,
-           xs, xr, ys, yr, zs, zr, gs, gr, in_sem, sem, ready):
+           lr, ms, fo, a_, u1, u2, u3, w0, w1, w2,
+           co, xs, xr, ys, yr, zs, zr, gs, gr, in_sem, sem, ready):
     nx, ny = sizes
     gz, gx, gy = lax.axis_index("gz"), lax.axis_index("gx"), lax.axis_index("gy")
     partner = {"gz": 1 - gz}
@@ -207,15 +218,7 @@
 
     def finish(i, _):
         z = source(i - 1)
-        weight, s1 = a_[i, 0, OWN], u1[i, 0, OWN]
-        c, n = stencil_own(u3, i)
-        s4 = s1 + weight * n
-        b, n = stencil_own(w2, i)
-        w3 = KEEP * b + weight * n
-        second = u2[i, 0, OWN]
-        total = w0[i, 0, OWN] * s4 + w1[i, 0, OWN] * (c - KEEP * second) + b * (second - KEEP * s1) + w3 * s1
-        rg[z] = (2.0 / RELAX) * jnp.exp(-2.0 * lr[z]) * total
-        it[z] = jnp.where(ms[z] > 0, KEEP * c + s4, LAND * fo[z])
+        it[z], rg[z] = last_step(i, z, lr, ms, fo, a_, u1, u2, u3, w0, w1, w2)
         return 0
 
     first = sweep(u1, u2, w0, w1)
@@ -286,7 +289,6 @@
 
     lax.fori_loop(16, 18, first, 0, unroll=True)
     lax.fori_loop(15, 18, second, 0, unroll=True)
-    lax.fori_loop(14, 17, finish, 0, unroll=True)
 
     for side in SIDES:
         @pl.when(has[side])
@@ -310,12 +312,11 @@
         field = pltpu.VMEM((19, 2, 48, 128), f32)
         return pl.pallas_call(
             functools.partial(kernel, sizes),
-            out_shape=[pltpu.VMEM(block, f32)] * 2,
+            out_shape=[pltpu.VMEM(block, f32)] * 3 + [pltpu.VMEM(block, jnp.int32), pltpu.VMEM(block, f32)] + [field] * 7,
             in_specs=[pl.BlockSpec(memory_space=pltpu.HBM)] * 4,
-            out_specs=[pl.BlockSpec(memory_space=pltpu.VMEM)] * 2,
+            out_specs=[pl.BlockSpec(memory_space=pltpu.VMEM)] * 12,
             scratch_shapes=[
-                pltpu.VMEM(block, f32), pltpu.VMEM(block, jnp.int32), pltpu.VMEM(block, f32), pltpu.VMEM(block, f32),
-                field, field, field, field, field, field, field,
+                pltpu.VMEM(block, f32),
                 pltpu.VMEM((2, 16, 8, 128), f32), pltpu.VMEM((2, 16, 8, 128), f32),
                 pltpu.VMEM((2, 32, 128), f32), pltpu.VMEM((2, 48, 128), f32),
                 pltpu.VMEM((5, 32, 128), f32), pltpu.VMEM((5, 32, 128), f32),
@@ -323,24 +324,34 @@
                 pltpu.SemaphoreType.DMA((4,)), pltpu.SemaphoreType.DMA((2, 12)),
                 pltpu.SemaphoreType.REGULAR,
             ],
-            compiler_params=pltpu.CompilerParams(collective_id=0, has_side_effects=True, vmem_limit_bytes=48 * 1024 * 1024),
+            compiler_params=pltpu.CompilerParams(collective_id=0, has_side_effects=True, vmem_limit_bytes=16 * 1024 * 1024),
             cost_estimate=pl.CostEstimate(flops=10_000_000, bytes_accessed=1_600_000, transcendentals=200_000),
         )(*(pltpu.with_memory_space_constraint(x, pltpu.HBM) for x in (log_range, sea_mask, forcing, cotangent)))
 
-    def store(it, rg, it_h, rg_h, sem):
-        copies = [pltpu.make_async_copy(v.at[pl.ds(16 * h, 16)], o.at[pl.ds(16 * h, 16)], sem.at[i, h])
-                  for i, (v, o) in enumerate(((it, it_h), (rg, rg_h))) for h in range(1)]
-        for copy in copies:
-            copy.start()
+    def store(it, rg, lr, ms, fo, a_, u1, u2, u3, w0, w1, w2, it_h, rg_h, last_it, last_rg, sem):
+        gz = lax.axis_index("gz")
+        bulk, start = pl.ds(3 * gz, 13), 13 * (1 - gz)
+        copies = [pltpu.make_async_copy(v, h, sem.at[i]) for i, (v, h) in enumerate((
+            (it.at[bulk], it_h.at[bulk]), (rg.at[bulk], rg_h.at[bulk]),
+            (last_it, it_h.at[pl.ds(start, 3)]), (last_rg, rg_h.at[pl.ds(start, 3)])))]
+        copies[0].start()
+        copies[1].start()
+        for i in range(14, 17):
+            z = jnp.where(gz == 0, i - 1, 16 - i)
+            last_it[z - start], last_rg[z - start] = last_step(i, z, lr, ms, fo, a_, u1, u2, u3, w0, w1, w2)
+        copies[2].start()
+        copies[3].start()
         for copy in copies:
             copy.wait()
 
     def whole(*args):
-        parts = body(*args)
-        parts = [pltpu.with_memory_space_constraint(x, pltpu.VMEM) for x in parts]
-        return pl.pallas_call(store, out_shape=[jax.ShapeDtypeStruct(x.shape, jnp.float32) for x in parts],
-                              in_specs=[pl.BlockSpec(memory_space=pltpu.VMEM)] * 2,
+        parts = [pltpu.with_memory_space_constraint(x, pltpu.VMEM) for x in body(*args)]
+        block = parts[0].shape
+        last = pltpu.VMEM((3, *block[1:]), jnp.float32)
+        return pl.pallas_call(store, out_shape=[jax.ShapeDtypeStruct(block, jnp.float32)] * 2,
+                              in_specs=[pl.BlockSpec(memory_space=pltpu.VMEM)] * 12,
                               out_specs=[pl.BlockSpec(memory_space=pl.ANY)] * 2,
-                              scratch_shapes=[pltpu.SemaphoreType.DMA((2, 1))])(*parts)
+                              scratch_shapes=[last, last, pltpu.SemaphoreType.DMA((4,))],
+                              compiler_params=pltpu.CompilerParams(vmem_limit_bytes=4 * 1024 * 1024))(*parts)
 
     return jax.shard_map(whole, mesh=mesh, in_specs=(spec,) * 4, out_specs=(spec, spec), check_vma=False)

time: 30.7 us -> 30.8 us (level)
  no operation moved by 1% of the time
where the time goes in v6:
time: 30.8 us; the launch traced here: 30.6 us
  Pallas kernels  30 us (97%)
  between operations  0.64 us (2%)
    pallas_call x1, Pallas kernels, body(): pl.pallas_call(functools.partial(kernel, sizes), out_shape=[pltpu.VMEM(bl...  29.1 us
    pallas_call x1, Pallas kernels, whole(): pl.pallas_call(store, out_shape=[jax.ShapeDtypeStruct(block, jnp.float32)...  0.92 us

profile of v6, /device:TPU:56, one launch (start us, length us, event | category | flops | bytes accessed | tf_op | source)
XLA Modules:
  0.0 30.6 jit_solution(3947891062692882661)
XLA Ops:
  0.6 29.1 %shard_map.59 = (f32[16,32,128]{2,1,0:T(8,128)S(1)}, f32[16,32,128]{2,1,0:T(8,128)S(1)}, f32[16,32,128]{2,1,0:T(8,128)S(1)}, s32[16,32,128]{2,1,0:T(8,128)S(1)},...) custom-call(f32[16,32,128]{2,1,0:T(8,128)} %lr_h.1, ...), custom_call_target="tpu_custom_call" | custom-call | flops 10000000 | bytes 1600000 | tf_op jit(solution)/shard_map/pallas_call | solution.py:313
  29.7 0.9 %shard_map.60 = (f32[16,32,128]{2,1,0:T(8,128)}, f32[16,32,128]{2,1,0:T(8,128)}) custom-call(f32[16,32,128]{2,1,0:T(8,128)S(1)} %get-tuple-element.14.it, f32[16,32,128]{2,1,0:T(8,128)S(1)} %get-tuple-element.15.rg, f32[16,32,128]{2,1,0:T(8,128)S(1)} %get-tuple-element.16.lr, s32[16,32,128]{2,1,0:T(8,128)S(1)} %get-tuple-element.17.ms, ...), custom_call_target="tpu_custom_call" | custom-call | tf_op jit(solution)/shard_map/pallas_call | solution.py:351

commit v7 on v5

--- a/solution.py
+++ b/solution.py
@@ -11,7 +11,7 @@
 SIDES = ((-1, -1), (1, -1), (-1, 1), (1, 1), (0, -1), (0, 1), (-1, 0), (1, 0))
 RELAX = 0.9
 KEEP = 1.0 - RELAX
-TURNS = (0, 0, 0, 0, 0, 3, 2, 2)
+TURNS = (0, 0, 0, 0, 0, 2, 2, 2)
 LAND = RELAX * (1.0 + KEEP + KEEP * KEEP + KEEP * KEEP * KEEP)
 OWN = pl.ds(8, 32)
 
@@ -161,7 +161,7 @@
             copies[side].start()
     send_layers(0)
     for side in far:
-        @pl.when(has[side])
+        @pl.when(has[side] & (gz == 0))
         def _():
             far[side].start()
 
@@ -249,10 +249,14 @@
     send_layers(2)
 
     for side in far:
+        @pl.when(has[side] & (gz == 1))
+        def _():
+            far[side].start()
+    send_layers(3)
+    for side in far:
         @pl.when(has[-side[0], -side[1]])
         def _():
             far[side].wait_recv()
-    send_layers(3)
     lax.fori_loop(3, 16, halo, carry)
     lax.fori_loop(1, 6, first, 0, unroll=5)
     send_layers(4)

time: 30.7 us -> 30.9 us (level)
  the two profiles are of different devices: /device:TPU:56 before, /device:TPU:185 now
where the time goes in v7:
time: 30.9 us; the launch traced here: 30.7 us
  Pallas kernels  30.1 us (97%)
  between operations  0.64 us (2%)
    pallas_call x1, Pallas kernels, body(): pl.pallas_call(functools.partial(kernel, sizes), out_shape=[pltpu.VMEM(bl...  29.3 us
    pallas_call x1, Pallas kernels, whole(): pl.pallas_call(store, out_shape=[jax.ShapeDtypeStruct(x.shape, jnp.float3...  0.81 us

profile of v7, /device:TPU:185, one launch (start us, length us, event | category | flops | bytes accessed | tf_op | source)
XLA Modules:
  0.0 30.7 jit_solution(4608912832274595811)
XLA Ops:
  0.6 29.3 %shard_map.59 = (f32[16,32,128]{2,1,0:T(8,128)S(1)}, f32[16,32,128]{2,1,0:T(8,128)S(1)}) custom-call(f32[16,32,128]{2,1,0:T(8,128)} %lr_h.1, s32[16,32,128]{2,1,0:T(8,128)} %m_h.1, f32[16,32,128]{2,1,0:T(8,128)} %f_h.1, f32[16,32,128]{2,1,0:T(8,128)} %c_h.1), custom_call_target="tpu_custom_call" | custom-call | flops 10000000 | bytes 1600000 | tf_op jit(solution)/shard_map/pallas_call | solution.py:315
  29.9 0.8 %shard_map.60 = (f32[16,32,128]{2,1,0:T(8,128)}, f32[16,32,128]{2,1,0:T(8,128)}) custom-call(f32[16,32,128]{2,1,0:T(8,128)S(1)} %get-tuple-element.4.it, f32[16,32,128]{2,1,0:T(8,128)S(1)} %get-tuple-element.5.rg), custom_call_target="tpu_custom_call" | custom-call | tf_op jit(solution)/shard_map/pallas_call | solution.py:345

commit v8 on v7

--- a/solution.py
+++ b/solution.py
@@ -161,7 +161,7 @@
             copies[side].start()
     send_layers(0)
     for side in far:
-        @pl.when(has[side] & (gz == 0))
+        @pl.when(has[side] & ((gz == 0) | (place > 2)))
         def _():
             far[side].start()
 
@@ -249,7 +249,7 @@
     send_layers(2)
 
     for side in far:
-        @pl.when(has[side] & (gz == 1))
+        @pl.when(has[side] & (gz == 1) & (place <= 2))
         def _():
             far[side].start()
     send_layers(3)

time: 30.9 us -> 30.6 us (level)
  no operation moved by 1% of the time
where the time goes in v8:
time: 30.6 us; the launch traced here: 30.5 us
  Pallas kernels  29.8 us (97%)
  between operations  0.64 us (2%)
    pallas_call x1, Pallas kernels, body(): pl.pallas_call(functools.partial(kernel, sizes), out_shape=[pltpu.VMEM(bl...  29 us
    pallas_call x1, Pallas kernels, whole(): pl.pallas_call(store, out_shape=[jax.ShapeDtypeStruct(x.shape, jnp.float3...  0.81 us

profile of v8, /device:TPU:185, one launch (start us, length us, event | category | flops | bytes accessed | tf_op | source)
XLA Modules:
  0.0 30.5 jit_solution(14228663801961176342)
XLA Ops:
  0.6 29.0 %shard_map.59 = (f32[16,32,128]{2,1,0:T(8,128)S(1)}, f32[16,32,128]{2,1,0:T(8,128)S(1)}) custom-call(f32[16,32,128]{2,1,0:T(8,128)} %lr_h.1, s32[16,32,128]{2,1,0:T(8,128)} %m_h.1, f32[16,32,128]{2,1,0:T(8,128)} %f_h.1, f32[16,32,128]{2,1,0:T(8,128)} %c_h.1), custom_call_target="tpu_custom_call" | custom-call | flops 10000000 | bytes 1600000 | tf_op jit(solution)/shard_map/pallas_call | solution.py:315
  29.7 0.8 %shard_map.60 = (f32[16,32,128]{2,1,0:T(8,128)}, f32[16,32,128]{2,1,0:T(8,128)}) custom-call(f32[16,32,128]{2,1,0:T(8,128)S(1)} %get-tuple-element.4.it, f32[16,32,128]{2,1,0:T(8,128)S(1)} %get-tuple-element.5.rg), custom_call_target="tpu_custom_call" | custom-call | tf_op jit(solution)/shard_map/pallas_call | solution.py:345
